TPU v7x, 32 devices: a whole 2x2x4 slice. The times are simulated.
32 devices in a mesh: seq: 8 (over y, x, core), head: 4 (over z).
Axes of the slice: x: 2, y: 2, z: 4, core: 2. Of those that a mesh axis runs over, the one named last changes fastest.
Arguments:
- queries: bfloat16 [4096, 64, 128], P('seq', 'head'), may hold values from -48 to 48
- keys_values: bfloat16 [4096, 2, 8, 128], P('seq'), may hold values from -6 to 6
- grad_out: bfloat16 [4096, 64, 128], P('seq', 'head'), may hold values from -6 to 6
- segments: int32 [4096], P('seq'), may hold values from 0 to 14, as said below
- partner: int32 [8], replicated, may hold values from 0 to 7, as said below
- prompt_blocks: int32 [8], replicated, may hold values from 1 to 4, as said below
Outputs:
- attention: bfloat16 [4096, 64, 128], P('seq', 'head')
- query_gradient: bfloat16 [4096, 64, 128], P('seq', 'head')
- kv_grad: bfloat16 [4096, 2048], P('seq', 'head')
Inputs may be any that keep to these rules, and one draw needn't show every extreme that they name: `segments`: within each bin ids never fall; segment 0 begins at the bin's first token and holds more than 64 tokens; segment 1 follows it directly and is the bin's rejected response; the largest id is reached in some bin in every draw. partner[b] != b, every bin is the partner of exactly one bin, and following partner from any bin visits all bins. `prompt_blocks`: the largest value is reached in every draw.
All inputs are finite; a program needn't handle non-finite values.
Results may differ from a plain program's by a relative error of at most 0.025.
Values may be sent and summed in bfloat16 or wider, within the bound.
A program may use at most 128 MiB of HBM per device.

v0:
```python
import math

import jax
import jax.numpy as jnp
from jax import lax
from jax.sharding import PartitionSpec as P

HEADS = 64
KVH = 8
PMAX = 64
BLK = 16


def from_partner(value, axis, apart):
    mask = 2**apart
    pairs = [(source, source ^ mask) for source in range(lax.axis_size(axis))]
    return lax.ppermute(value, axis, pairs)


def slotted(parcel, wanted):
    mask = wanted.reshape((-1,) + (1,) * parcel.ndim)
    return jnp.where(mask, parcel[None], jnp.zeros((), parcel.dtype))


def head_total(block, sharing):
    flat = block.reshape(block.shape[0], -1)
    place = lax.axis_index("head")
    for bit in reversed(range(sharing.bit_length() - 1)):
        half = flat.shape[1] // 2
        mine = place // 2**bit % 2
        kept = lax.dynamic_slice_in_dim(flat, mine * half, half, 1)
        given = lax.dynamic_slice_in_dim(flat, (1 - mine) * half, half, 1)
        got = from_partner(given.astype(jnp.bfloat16), "head", bit).astype(given.dtype)
        flat = kept + got
    return flat


def body(queries, keys_values, grad_out, segments, partner, prompt_blocks):
    rows_here = queries.shape[0]
    heads_here = queries.shape[1]
    head_dim = queries.shape[2]
    group_size = HEADS // KVH
    kv_here = max(1, heads_here // group_size)
    per_kv = heads_here // kv_here
    sharing = max(1, group_size // heads_here)
    kv_start = lax.axis_index("head") * heads_here // group_size
    self_index = lax.axis_index("seq")
    bin_count = lax.axis_size("seq")
    score_scaling = 1.0 / math.sqrt(head_dim)
    bin_ids = jnp.arange(bin_count, dtype=jnp.int32)
    owner_bin = partner[self_index]
    source = jnp.sum(jnp.where(partner == self_index, bin_ids, 0))
    kv_local = lax.dynamic_slice_in_dim(keys_values, kv_start, kv_here, 2)
    prompt = kv_local[:PMAX]
    received = lax.all_to_all(
        slotted(prompt, partner == self_index), "seq", split_axis=0, concat_axis=0, tiled=True
    )
    remote = lax.dynamic_index_in_dim(received, owner_bin, 0, keepdims=False)
    every_key_row = jnp.concatenate([kv_local[:, 0], remote[:, 0]], axis=0)
    every_value_row = jnp.concatenate([kv_local[:, 1], remote[:, 1]], axis=0)
    query_by_group = queries.reshape(rows_here, kv_here, per_kv, head_dim)
    gradient_by_group = grad_out.reshape(rows_here, kv_here, per_kv, head_dim)
    positions = jnp.arange(rows_here, dtype=jnp.int32)
    local_ok = (segments[:, None] == segments[None, :]) & (positions[None, :] <= positions[:, None])
    live_count = BLK * prompt_blocks[owner_bin]
    remote_ok = (segments[:, None] == 1) & (jnp.arange(PMAX, dtype=jnp.int32)[None, :] < live_count)
    allowed = jnp.concatenate([local_ok, remote_ok], axis=1)[None, None]
    score_matrix = (
        jnp.einsum(
            "imwh,lmh->mwil", query_by_group, every_key_row, preferred_element_type=jnp.float32
        )
        * score_scaling
    )
    score_matrix = jnp.where(allowed, score_matrix, -jnp.inf)
    row_peak = jnp.max(score_matrix, axis=-1, keepdims=True)
    weights_raw = jnp.where(allowed, jnp.exp(score_matrix - row_peak), jnp.float32(0.0))
    probabilities = weights_raw / jnp.sum(weights_raw, axis=-1, keepdims=True)
    probability_lowprec = probabilities.astype(jnp.bfloat16)
    blended_values = jnp.einsum(
        "aqiu,uax->iaqx", probability_lowprec, every_value_row, preferred_element_type=jnp.float32
    )
    attention = blended_values.astype(jnp.bfloat16)
    row_delta = jnp.sum(
        gradient_by_group.astype(jnp.float32) * attention.astype(jnp.float32), axis=-1
    )
    row_delta = jnp.transpose(row_delta, (1, 2, 0))
    probability_gradient = jnp.einsum(
        "imwh,lmh->mwil", gradient_by_group, every_value_row, preferred_element_type=jnp.float32
    )
    score_gradient = (probabilities * (probability_gradient - row_delta[..., None])).astype(
        jnp.bfloat16
    )
    query_gradient = (
        jnp.einsum(
            "aqiu,uax->iaqx", score_gradient, every_key_row, preferred_element_type=jnp.float32
        )
        * score_scaling
    )
    query_gradient = query_gradient.astype(jnp.bfloat16).reshape(rows_here, heads_here, head_dim)
    key_grad = (
        jnp.einsum(
            "emox,oemn->xen", score_gradient, query_by_group, preferred_element_type=jnp.float32
        )
        * score_scaling
    )
    value_grad = jnp.einsum(
        "emox,oemn->xen", probability_lowprec, gradient_by_group, preferred_element_type=jnp.float32
    )
    kv_grads = jnp.stack([key_grad, value_grad], axis=2).astype(jnp.bfloat16)
    local_part = kv_grads[:rows_here]
    remote_part = kv_grads[rows_here:]
    received_grads = lax.all_to_all(
        slotted(remote_part, bin_ids == owner_bin), "seq", split_axis=0, concat_axis=0, tiled=True
    )
    arrived = lax.dynamic_index_in_dim(received_grads, source, 0, keepdims=False)
    joined = lax.optimization_barrier(jnp.concatenate([local_part, arrived], axis=0))
    summed = head_total(joined.astype(jnp.float32), sharing)
    own_sum = summed[:rows_here]
    prompt_low = summed[rows_here:].astype(jnp.bfloat16)
    prompt_rows = own_sum[:PMAX] + prompt_low.astype(jnp.float32)
    kv_result = jnp.concatenate([prompt_rows, own_sum[PMAX:]], axis=0).astype(jnp.bfloat16)
    return (attention.reshape(rows_here, heads_here, head_dim), query_gradient, kv_result)


def solution(mesh):
    in_specs = (
        P("seq", "head", None),
        P("seq", None, None, None),
        P("seq", "head", None),
        P("seq"),
        P(),
        P(),
    )
    out_specs = (P("seq", "head", None), P("seq", "head", None), P("seq", "head"))
    return jax.shard_map(body, mesh=mesh, in_specs=in_specs, out_specs=out_specs, check_vma=False)
```

profile of v0, /device:TPU:0, one launch (start us, length us, event | category | flops | bytes accessed | tf_op | source)
XLA Modules:
  0.0 110.2 jit_solution(15032972988035299688)
XLA Ops:
  0.7 1.2 %constant_dynamic-slice_fusion = bf16[64,2,2,128]{3,2,1,0:T(2,128)(2,1)S(1)} fusion(bf16[512,2,8,128]{3,2,1,0:T(8,128)(2,1)} %param.7, s32[]{:T(128)S(6)} %select_n.39), kind=kLoop, calls=%fused_computation.47 | loop fusion | bytes 131076 | tf_op jit(solution)/shard_map/slice | solution.py:54
  1.9 1.4 %select_reduce_fusion = (s32[]{:T(128)}, pred[8]{0:T(512)(128)(4,1)S(1)}) fusion(s32[8]{0:T(128)} %param.10, s32[]{:T(128)S(6)} %axis_index.25), kind=kLoop, calls=%fused_computation.52 | loop fusion | flops 23 | bytes 48 | tf_op jit(solution)/shard_map/reduce_sum | solution.py:52
  3.2 0.9 broadcast_select_fusion.1
  4.1 5.2 %all-to-all-start = ((bf16[8,64,2,2,128]{4,1,3,2,0:T(8,128)(2,1)}), bf16[8,64,2,2,128]{4,1,3,2,0:T(8,128)(2,1)S(1)}, u32[]{:S(2)}, u32[]{:S(2)}) async-start(bf16[8,64,2,2,128]{4,1,3,2,0:T(8,128)(2,1)} %broadcast_select_fusion.1), calls=%async_computation | async-start | bytes 1048576 | tf_op jit(solution)/shard_map/all_to_all | solution.py:55
  9.3 1.3 %dynamic_slice.17 = s32[1]{0:T(128)} dynamic-slice(s32[8]{0:T(128)} %param.10, s32[]{:T(128)S(6)} %select_n.41), dynamic_slice_sizes={1} | dynamic-slice | bytes 12 | tf_op jit(solution)/shard_map/dynamic_slice | solution.py:51
  11.8 0.7 broadcast_compare_fusion
  12.5 1.0 fusion.26
  14.7 4.3 %copy.21 = bf16[512,16,128]{0,2,1:T(8,128)(2,1)} copy(bf16[512,16,128]{2,1,0:T(8,128)(2,1)} %param.8) | data formatting | bytes 4194304 | tf_op args[2]
  19.6 1.2 %dynamic_slice.19 = s32[1]{0:T(128)} dynamic-slice(s32[8]{0:T(128)} %param.11, s32[]{:T(128)S(6)} %select_n.42), dynamic_slice_sizes={1} | dynamic-slice | bytes 12 | tf_op jit(solution)/shard_map/dynamic_slice | solution.py:65
  21.5 4.3 %copy.33 = bf16[512,2,8,128]{0,3,2,1:T(8,128)(2,1)} copy(bf16[512,2,8,128]{3,2,1,0:T(8,128)(2,1)} %bitcast.89) | data formatting | bytes 4194304 | tf_op jit(solution)/shard_map/reshape | solution.py:62
  25.8 0.1 broadcast_and_fusion
  26.5 0.6 iota_compare_fusion.1
  27.1 2.1 %constant_dynamic-slice_fusion.1 = (bf16[512,1,2,128]{3,2,1,0:T(2,128)(2,1)S(1)}, bf16[512,1,2,128]{3,2,1,0:T(2,128)(2,1)S(1)}) fusion(bf16[512,2,8,128]{3,2,1,0:T(8,128)(2,1)} %param.7, s32[]{:T(128)S(6)} %add.28, s32[]{:T(128)S(6)} %select_n.39), kind=kLoop, calls=%fused_computation.48 | loop fusion | bytes 1048584 | tf_op jit(solution)/shard_map/slice | solution.py:60
  29.2 0.1 copy_bitcast_fusion
  29.4 9.1 %fusion.10 = f32[2,576,512,8]{2,1,3,0:T(8,128)} fusion(bf16[512,2,8,128]{3,2,1,0:T(8,128)(2,1)S(1)} %bitcast.87, bf16[64,2,128]{2,0,1:T(8,128)(2,1)S(1)} %get-tuple-element.14, bf16[512,2,128]{2,0,1:T(8,128)(2,1)S(1)} %get-tuple-element.19), kind=kOutput, calls=%fused_computation.17 | convolution fusion | flops 1208549376 | bytes 21266432 | tf_op jit(solution)/shard_map/imwh,lmh->mwil/dot_general | solution.py:69
  38.5 19.9 %fusion.34 = (f32[2,8,512]{2,1,0:T(8,128)S(1)}, f32[2,8,512,576]{2,3,1,0:T(8,128)}) fusion(f32[2,576,512,8]{2,1,3,0:T(8,128)} %fusion.10, pred[512,576]{0,1:T(8,128)(4,1)S(1)} %pad_add_fusion), kind=kOutput, calls=%fused_computation.62 | output fusion | flops 33030720 | bytes 38076416 | tf_op jit(solution)/shard_map/sub | solution.py:76
  58.4 7.5 %fusion.7 = bf16[2,8,512,576]{2,3,1,0:T(8,128)(2,1)S(1)} fusion(f32[2,8,512,576]{2,3,1,0:T(8,128)} %get-tuple-element.16, f32[2,8,512]{2,1,0:T(8,128)S(1)} %get-tuple-element.15), kind=kLoop, calls=%fused_computation.11 | loop fusion | flops 9437184 | bytes 28344320 | tf_op jit(solution)/shard_map/convert_element_type | solution.py:78
  65.9 2.6 %fusion.25 = bf16[576,2,1,128]{3,0,1,2:T(8,128)(2,1)S(1)} fusion(bf16[2,8,512,576]{2,3,1,0:T(8,128)(2,1)S(1)} %fusion.7, bf16[512,2,8,128]{0,3,2,1:T(8,128)(2,1)S(1)} %copy-done.3), kind=kOutput, calls=%fused_computation.26 | convolution fusion | flops 1208107008 | bytes 11829248 | tf_op jit(solution)/shard_map/emox,oemn->xen/dot_general | solution.py:106
  68.5 3.2 %multiply_reduce_fusion = (f32[512,2,8]{0,2,1:T(8,128)S(1)}, bf16[2,128,8,512]{3,1,2,0:T(8,128)(2,1)}) fusion(bf16[512,2,8,128]{0,3,2,1:T(8,128)(2,1)S(1)} %bitcast.90, bf16[2,8,512,576]{2,3,1,0:T(8,128)(2,1)S(1)} %fusion.7, bf16[64,2,128]{2,0,1:T(8,128)(2,1)S(1)} %get-tuple-element.13, bf16[512,2,128]{2,0,1:T(8,128)(2,1)S(1)} %get-tuple-element.20), kind=kOutput, calls=%fused_computation.13 | convolution fusion | flops 1213784064 | bytes 13959168 | tf_op jit(solution)/shard_map/aqiu,uax->iaqx/dot_general | solution.py:79
  71.8 8.5 %fusion.2 = bf16[2,8,512,576]{2,3,1,0:T(8,128)(2,1)S(1)} fusion(f32[2,8,512]{2,1,0:T(8,128)S(1)} %bitcast.93, f32[2,8,512,576]{2,3,1,0:T(8,128)} %get-tuple-element.16, f32[2,8,512]{2,1,0:T(8,128)S(1)} %get-tuple-element.15, bf16[512,2,8,128]{0,3,2,1:T(8,128)(2,1)} %copy.33, bf16[64,2,128]{2,0,1:T(8,128)(2,1)S(1)} %get-tuple-element.13, ...), kind=kOutput, calls=%fused_computation.3 | convolution fusion | flops 1227423744 | bytes 30769152 | tf_op jit(solution)/shard_map/imwh,lmh->mwil/dot_general | solution.py:87
  80.3 3.6 %copy-done.1 = bf16[2,8,512,576]{2,3,1,0:T(8,128)(2,1)} copy-done((bf16[2,8,512,576]{2,3,1,0:T(8,128)(2,1)}, bf16[2,8,512,576]{2,3,1,0:T(8,128)(2,1)S(1)}, u32[]{:S(2)}) %copy-start.1) | copy-done | bytes 9437208
  83.9 2.6 %fusion.22 = bf16[576,2,1,128]{3,0,1,2:T(8,128)(2,1)S(1)} fusion(bf16[2,8,512,576]{2,3,1,0:T(8,128)(2,1)S(1)} %fusion.2, bf16[512,2,8,128]{3,2,1,0:T(8,128)(2,1)S(1)} %bitcast.88), kind=kOutput, calls=%fused_computation.25 | convolution fusion | flops 1208254464 | bytes 11829248 | tf_op jit(solution)/shard_map/emox,oemn->xen/dot_general | solution.py:101
  86.5 1.0 broadcast_select_fusion
  87.5 4.2 %all-to-all-start.1 = ((bf16[8,64,2,2,128]{4,1,3,2,0:T(8,128)(2,1)}), bf16[8,64,2,2,128]{4,1,3,2,0:T(8,128)(2,1)}, u32[]{:S(2)}, u32[]{:S(2)}) async-start(bf16[8,64,2,2,128]{4,1,3,2,0:T(8,128)(2,1)} %broadcast_select_fusion), calls=%async_computation.1 | async-start | bytes 1048576 | tf_op jit(solution)/shard_map/all_to_all | solution.py:112
  91.7 6.9 %multiply_convert_fusion = bf16[2,128,8,512]{3,1,2,0:T(8,128)(2,1)} fusion(bf16[2,8,512,576]{2,3,1,0:T(8,128)(2,1)} %copy-done.1, bf16[64,2,128]{2,0,1:T(8,128)(2,1)S(1)} %get-tuple-element.14, bf16[512,2,128]{2,0,1:T(8,128)(2,1)S(1)} %get-tuple-element.19), kind=kOutput, calls=%fused_computation.12 | convolution fusion | flops 1210646528 | bytes 11829248 | tf_op jit(solution)/shard_map/aqiu,uax->iaqx/dot_general | solution.py:94
  98.5 4.5 %copy.29 = bf16[512,16,128]{2,1,0:T(8,128)(2,1)} copy(bf16[512,16,128]{0,2,1:T(8,128)(2,1)} %bitcast.91) | data formatting | bytes 4194304
  103.0 4.5 %copy.30 = bf16[512,16,128]{2,1,0:T(8,128)(2,1)} copy(bf16[512,16,128]{0,2,1:T(8,128)(2,1)} %bitcast.92) | data formatting | bytes 4194304
  107.6 0.9 copy_bitcast_fusion.2
  108.6 0.5 copy.28
  109.0 0.2 slice.55
  109.2 0.1 copy.27
  109.3 0.8 pad_maximum_fusion.1
  (19 shorter events, 0.3 us)
Async XLA Ops:
  0.6 28.7 %copy-start = (bf16[512,16,128]{2,1,0:T(8,128)(2,1)S(1)}, bf16[512,16,128]{2,1,0:T(8,128)(2,1)}, u32[]{:S(2)}) copy-start(bf16[512,16,128]{2,1,0:T(8,128)(2,1)} %param.6) | copy-start | bytes 6291460
  4.1 25.2 %all-to-all-start = ((bf16[8,64,2,2,128]{4,1,3,2,0:T(8,128)(2,1)}), bf16[8,64,2,2,128]{4,1,3,2,0:T(8,128)(2,1)S(1)}, u32[]{:S(2)}, u32[]{:S(2)}) async-start(bf16[8,64,2,2,128]{4,1,3,2,0:T(8,128)(2,1)} %broadcast_select_fusion.1), calls=%async_computation | async-start | bytes 1048576 | tf_op jit(solution)/shard_map/all_to_all | solution.py:55
  58.4 7.5 %copy-start.3 = (bf16[512,2,8,128]{0,3,2,1:T(8,128)(2,1)S(1)}, bf16[512,2,8,128]{0,3,2,1:T(8,128)(2,1)}, u32[]{:S(2)}) copy-start(bf16[512,2,8,128]{0,3,2,1:T(8,128)(2,1)} %copy.33) | copy-start | bytes 6291460
  65.9 2.6 %copy-start.2 = (bf16[512,16,128]{0,2,1:T(8,128)(2,1)S(1)}, bf16[512,16,128]{0,2,1:T(8,128)(2,1)}, u32[]{:S(2)}) copy-start(bf16[512,16,128]{0,2,1:T(8,128)(2,1)} %copy.21) | copy-start | bytes 6291460
  80.3 3.6 %copy-start.1 = (bf16[2,8,512,576]{2,3,1,0:T(8,128)(2,1)}, bf16[2,8,512,576]{2,3,1,0:T(8,128)(2,1)S(1)}, u32[]{:S(2)}) copy-start(bf16[2,8,512,576]{2,3,1,0:T(8,128)(2,1)S(1)} %fusion.2) | copy-start | bytes 28311556
  87.5 20.1 %all-to-all-start.1 = ((bf16[8,64,2,2,128]{4,1,3,2,0:T(8,128)(2,1)}), bf16[8,64,2,2,128]{4,1,3,2,0:T(8,128)(2,1)}, u32[]{:S(2)}, u32[]{:S(2)}) async-start(bf16[8,64,2,2,128]{4,1,3,2,0:T(8,128)(2,1)} %broadcast_select_fusion), calls=%async_computation.1 | async-start | bytes 1048576 | tf_op jit(solution)/shard_map/all_to_all | solution.py:112
where the time goes:
time: 111 us; the launch traced here: 110 us
  other arithmetic  33.9 us (31%)
  matrix products  32.9 us (30%)
  local copies, waits for them, and re-layouts  28.7 us (26%)
  starting transfers between devices  9.37 us (8%)
  between operations  5.26 us (5%)
    sub x1, other arithmetic, body(): score_matrix - row_peak  19.9 us
    unnamed x12, local copies, waits for them, and re-layouts  16.9 us
    dot_general x1, matrix products, body(): jnp.einsum('imwh,lmh->mwil', query_by_group, every_key_row, preferred_ele...  9.12 us
    dot_general x1, matrix products, body(): jnp.einsum('imwh,lmh->mwil', gradient_by_group, every_value_row, preferre...  8.5 us
    convert_element_type x1, other arithmetic, body(): probability_lowprec = probabilities.astype(jnp.bfloat16)  7.52 us
    dot_general x1, matrix products, body(): jnp.einsum('aqiu,uax->iaqx', score_gradient, every_key_row, preferred_ele...  6.85 us
    all_to_all x1, starting transfers between devices, body(): lax.all_to_all(slotted(prompt, partner == self_index), 'seq', split_axis=...  5.17 us
    reshape x1, local copies, waits for them, and re-layouts, body(): gradient_by_group = grad_out.reshape(rows_here, kv_here, per_kv, head_dim)  4.27 us
  transfers between devices with their start and end apart: 2, of which 0 were waited for; matrix products, arithmetic and copies ran while one was open for 29% of the time, Pallas kernels for 0%

commit v1 on v0

v1 whole, which is shorter than its diff:
```python
import functools
import math

import jax
import jax.numpy as jnp
from jax import lax
from jax.experimental import pallas as pl
from jax.experimental.pallas import tpu as pltpu
from jax.sharding import PartitionSpec as P

HEADS = 64
KVH = 8
PMAX = 64
BLK = 16
ROWS = 128
PAD = 128
MASKED = -1e30
LOG2E = math.log2(math.e)


def from_partner(value, axis, apart):
    mask = 2**apart
    pairs = [(source, source ^ mask) for source in range(lax.axis_size(axis))]
    return lax.ppermute(value, axis, pairs)


def slotted(parcel, wanted):
    mask = wanted.reshape((-1,) + (1,) * parcel.ndim)
    return jnp.where(mask, parcel[None], jnp.zeros((), parcel.dtype))


def head_total(block, sharing):
    flat = block.reshape(block.shape[0], -1)
    place = lax.axis_index("head")
    for bit in reversed(range(sharing.bit_length() - 1)):
        half = flat.shape[1] // 2
        mine = place // 2**bit % 2
        kept = lax.dynamic_slice_in_dim(flat, mine * half, half, 1)
        given = lax.dynamic_slice_in_dim(flat, (1 - mine) * half, half, 1)
        got = from_partner(given.astype(jnp.bfloat16), "head", bit).astype(given.dtype)
        flat = kept + got
    return flat


def dot(a, b):
    return jnp.dot(a, b, preferred_element_type=jnp.float32)


def dot_t(a, b):
    return lax.dot_general(a, b, (((1,), (1,)), ((), ())), preferred_element_type=jnp.float32)


def attend(
    heads, kvs, per_kv, chunks, scale,
    partner_ref, blocks_ref, q_ref, do_ref, kv_ref, seg_ref, got_ref,
    out_ref, dq_ref, own_ref, prompt_ref,
    qf, dof, af, dqf, kvf, kcat, vcat, segc, bias, dkt, dvt,
):
    chunk = pl.program_id(0)
    me = lax.axis_index("seq")
    rows = chunks * ROWS
    width = PAD + rows

    @pl.when(chunk == 0)
    def _():
        owner = partner_ref[me]
        kv_start = lax.axis_index("head") * heads // (HEADS // KVH)
        step = ROWS * 2 * KVH
        for part in range(chunks):
            kvf[part * step:(part + 1) * step, :] = kv_ref[part * step:(part + 1) * step, :].astype(jnp.float32)
        for g in range(kvs):
            k_rows = kvf[pl.ds(kv_start + g, rows, stride=2 * KVH), :]
            v_rows = kvf[pl.ds(kv_start + g + KVH, rows, stride=2 * KVH), :]
            kcat[g, PAD:, :] = k_rows.astype(jnp.bfloat16)
            vcat[g, PAD:, :128] = v_rows.astype(jnp.bfloat16)
            kcat[g, PMAX:PAD, :] = jnp.zeros((PAD - PMAX, 128), jnp.bfloat16)
            vcat[g, PMAX:PAD, :128] = jnp.zeros((PAD - PMAX, 128), jnp.bfloat16)
            kcat[g, :PMAX, :] = got_ref[owner, g * PMAX:(g + 1) * PMAX, :]
            vcat[g, :PMAX, :128] = got_ref[owner, (kvs + g) * PMAX:(kvs + g + 1) * PMAX, :]
            vcat[g, :, 128:] = jnp.ones((width, 128), jnp.bfloat16)
        segc[...] = jnp.broadcast_to(seg_ref[...].astype(jnp.float32), (128, rows)).T
        dkt[...] = jnp.zeros_like(dkt)
        dvt[...] = jnp.zeros_like(dvt)

    qf[...] = q_ref[...].astype(jnp.float32)
    dof[...] = do_ref[...].astype(jnp.float32)

    def work(c):
        wide = PAD + (c + 1) * ROWS
        live = BLK * blocks_ref[partner_ref[me]]
        column = segc[c * ROWS:(c + 1) * ROWS, :]
        place = lax.broadcasted_iota(jnp.int32, (ROWS, 128), 1)
        row = lax.broadcasted_iota(jnp.int32, (ROWS, 128), 0)
        bias[:, :PAD] = jnp.where((column == 1.0) & (place < live), 0.0, MASKED)
        for j in range(c + 1):
            same = column == seg_ref[:, j * ROWS:(j + 1) * ROWS].astype(jnp.float32)
            if j == c:
                same = same & (place <= row)
            bias[:, PAD + j * ROWS:PAD + (j + 1) * ROWS] = jnp.where(same, 0.0, MASKED)

        def pair(i, carry):
            h = 2 * i
            g = h // per_kv
            first, second = pl.ds(h, ROWS, stride=heads), pl.ds(h + 1, ROWS, stride=heads)
            q32 = jnp.concatenate([qf[first, :], qf[second, :]], axis=0)
            q = q32.astype(jnp.bfloat16)
            k = kcat[g, :wide, :]
            s = dot_t(q, k) * (scale * LOG2E)
            b = bias[:, :wide]
            t = s + jnp.concatenate([b, b], axis=0)
            p = jnp.exp2(t - jnp.max(t, axis=1, keepdims=True))
            pb = p.astype(jnp.bfloat16)
            mixed = dot(pb, vcat[g, :wide, :])
            inverse = 1.0 / mixed[:, 128:]
            attention = (mixed[:, :128] * inverse).astype(jnp.bfloat16).astype(jnp.float32)
            af[first, :] = attention[:ROWS]
            af[second, :] = attention[ROWS:]
            do = jnp.concatenate([dof[first, :], dof[second, :]], axis=0)
            dos = (do * inverse).astype(jnp.bfloat16)
            dos32 = dos.astype(jnp.float32)
            delta = jnp.sum(dos32 * attention, axis=1, keepdims=True)
            dp = dot_t(dos, vcat[g, :wide, :128])
            ds = (p * (dp - delta)).astype(jnp.bfloat16)
            dq = dot(ds, k) * scale
            dqf[first, :] = dq[:ROWS]
            dqf[second, :] = dq[ROWS:]
            dkt[g, :, :wide] += dot(q32.T.astype(jnp.bfloat16), ds)
            dvt[g, :, :wide] += dot(dos32.T.astype(jnp.bfloat16), pb)
            return carry

        lax.fori_loop(0, heads // 2, pair, 0, unroll=2)

    for c in range(chunks):
        pl.when(chunk == c)(functools.partial(work, c))
    out_ref[...] = af[...].astype(jnp.bfloat16)
    dq_ref[...] = dqf[...].astype(jnp.bfloat16)

    @pl.when(chunk == chunks - 1)
    def _():
        for g in range(kvs):
            for part, grads in ((0, dkt[g] * scale), (1, dvt[g])):
                turned = grads.T.astype(jnp.bfloat16)
                at = (2 * g + part) * 128
                own_ref[:, at:at + 128] = turned[PAD:]
                prompt_ref[:, at:at + 128] = turned[:PMAX]


def body(queries, keys_values, grad_out, segments, partner, prompt_blocks):
    rows_here, heads_here, head_dim = queries.shape
    group_size = HEADS // KVH
    kv_here = max(1, heads_here // group_size)
    per_kv = heads_here // kv_here
    sharing = max(1, group_size // heads_here)
    kv_start = lax.axis_index("head") * heads_here // group_size
    self_index = lax.axis_index("seq")
    bin_count = lax.axis_size("seq")
    chunks = rows_here // ROWS
    width = PAD + rows_here
    bin_ids = jnp.arange(bin_count, dtype=jnp.int32)
    owner_bin = partner[self_index]
    source = jnp.sum(jnp.where(partner == self_index, bin_ids, 0))
    prompt = lax.dynamic_slice_in_dim(keys_values[:PMAX], kv_start, kv_here, 2)
    parcel = jnp.transpose(prompt, (1, 2, 0, 3)).reshape(2 * kv_here * PMAX, head_dim)
    received = lax.all_to_all(
        slotted(parcel, partner == self_index), "seq", split_axis=0, concat_axis=0, tiled=True
    )
    block = pl.BlockSpec((ROWS * heads_here, head_dim), lambda c: (c, 0))
    whole = pl.BlockSpec(memory_space=pltpu.VMEM)
    flat = jax.ShapeDtypeStruct((rows_here * heads_here, head_dim), jnp.bfloat16)
    f32, bf16 = jnp.float32, jnp.bfloat16
    attention, query_gradient, own, prompt_grad = pl.pallas_call(
        functools.partial(attend, heads_here, kv_here, per_kv, chunks, 1.0 / math.sqrt(head_dim)),
        grid=(chunks,),
        in_specs=[pl.BlockSpec(memory_space=pltpu.SMEM)] * 2 + [block, block, whole, whole, whole],
        out_specs=[block, block, whole, whole],
        out_shape=[
            flat,
            flat,
            jax.ShapeDtypeStruct((rows_here, kv_here * 2 * head_dim), bf16),
            jax.ShapeDtypeStruct((PMAX, kv_here * 2 * head_dim), bf16),
        ],
        scratch_shapes=[pltpu.VMEM((ROWS * heads_here, head_dim), f32)] * 4
        + [
            pltpu.VMEM((rows_here * 2 * KVH, head_dim), f32),
            pltpu.VMEM((kv_here, width, head_dim), bf16),
            pltpu.VMEM((kv_here, width, 2 * head_dim), bf16),
            pltpu.VMEM((rows_here, 128), f32),
            pltpu.VMEM((ROWS, width), f32),
            pltpu.VMEM((kv_here, head_dim, width), f32),
            pltpu.VMEM((kv_here, head_dim, width), f32),
        ],
        compiler_params=pltpu.CompilerParams(vmem_limit_bytes=40 * 2**20),
    )(
        partner,
        prompt_blocks,
        queries.reshape(-1, head_dim),
        grad_out.reshape(-1, head_dim),
        keys_values.reshape(-1, head_dim),
        segments.reshape(1, rows_here),
        received,
    )
    received_grads = lax.all_to_all(
        slotted(prompt_grad, bin_ids == owner_bin), "seq", split_axis=0, concat_axis=0, tiled=True
    )
    arrived = lax.dynamic_index_in_dim(received_grads, source, 0, keepdims=False)
    if sharing > 1:
        joined = lax.optimization_barrier(jnp.concatenate([own, arrived], axis=0))
        summed = head_total(joined.astype(jnp.float32), sharing)
        own, arrived = summed[:rows_here], summed[rows_here:].astype(jnp.bfloat16)
    head_rows = own[:PMAX].astype(jnp.float32) + arrived.astype(jnp.float32)
    kv_result = lax.dynamic_update_slice(own.astype(jnp.bfloat16), head_rows.astype(jnp.bfloat16), (0, 0))
    return (attention.reshape(queries.shape), query_gradient.reshape(queries.shape), kv_result)


def solution(mesh):
    in_specs = (
        P("seq", "head", None),
        P("seq", None, None, None),
        P("seq", "head", None),
        P("seq"),
        P(),
        P(),
    )
    out_specs = (P("seq", "head", None), P("seq", "head", None), P("seq", "head"))
    return jax.shard_map(body, mesh=mesh, in_specs=in_specs, out_specs=out_specs, check_vma=False)
```

time: 111 us -> 69.9 us (0.63)
  matrix products: 32.9 us -> 0 us
  Pallas kernels: 0 us -> 31.7 us
  other arithmetic: 33.9 us -> 5.26 us
  local copies, waits for them, and re-layouts: 28.7 us -> 4.98 us
  waiting for transfers between devices: 0.01 us -> 16.3 us
  between operations: 5.26 us -> 2.65 us
    dot_general x6 -> x0, matrix products: 32.9 us -> none  [the longest x1 9.12 us: body(): jnp.einsum('imwh,lmh->mwil', query_by_group, every_key_row, preferred_ele...]
    pallas_call x0 -> x1, Pallas kernels: none -> 31.7 us  [body(): pl.pallas_call(functools.partial(attend, heads_here, kv_here, per_kv, chu...]
    sub x1 -> x0, other arithmetic: 19.9 us -> none  [body(): score_matrix - row_peak]
    all_to_all x2, waiting for transfers between devices: 0.01 us -> 16.3 us  [the longest x1 8.49 us: body(): lax.all_to_all(slotted(parcel, partner == self_index), 'seq', split_axis=...]
    unnamed x12 -> x13, local copies, waits for them, and re-layouts: 16.9 us -> 3.21 us
    convert_element_type x1 -> x0, other arithmetic: 7.52 us -> none  [body(): probability_lowprec = probabilities.astype(jnp.bfloat16)]
    reshape x1 -> x0, local copies, waits for them, and re-layouts: 4.27 us -> none  [body(): gradient_by_group = grad_out.reshape(rows_here, kv_here, per_kv, head_dim)]
    slice x5 -> x1, local copies, waits for them, and re-layouts: 3.94 us -> 1.11 us  [body(): prompt = lax.dynamic_slice_in_dim(keys_values[:PMAX], kv_start, kv_here, 2)]
  transfers between devices with their start and end apart: 2 -> 2, of which waited for: 0 -> 2; matrix products, arithmetic and copies ran while one was open for 29% -> 2% of each run, Pallas kernels for 0% -> 0%
where the time goes in v1:
time: 69.9 us; the launch traced here: 69.5 us
  Pallas kernels  31.7 us (45%)
  waiting for transfers between devices  16.3 us (23%)
  starting transfers between devices  8.66 us (12%)
  other arithmetic  5.26 us (8%)
  local copies, waits for them, and re-layouts  4.98 us (7%)
  between operations  2.65 us (4%)
    pallas_call x1, Pallas kernels, body(): pl.pallas_call(functools.partial(attend, heads_here, kv_here, per_kv, chu...  31.7 us
    all_to_all x1, waiting for transfers between devices, body(): lax.all_to_all(slotted(parcel, partner == self_index), 'seq', split_axis=...  8.49 us
    all_to_all x1, waiting for transfers between devices, body(): lax.all_to_all(slotted(prompt_grad, bin_ids == owner_bin), 'seq', split_a...  7.77 us
    all_to_all x1, starting transfers between devices, body(): lax.all_to_all(slotted(parcel, partner == self_index), 'seq', split_axis=...  5.17 us
    all_to_all x1, starting transfers between devices, body(): lax.all_to_all(slotted(prompt_grad, bin_ids == owner_bin), 'seq', split_a...  3.49 us
    unnamed x13, local copies, waits for them, and re-layouts  3.21 us
    select_n x2, other arithmetic, slotted(): return jnp.where(mask, parcel[None], jnp.zeros((), parcel.dtype))  1.8 us
    dynamic_update_slice x1, other arithmetic, body(): lax.dynamic_update_slice(own.astype(jnp.bfloat16), head_rows.astype(jnp.b...  1.49 us
  transfers between devices with their start and end apart: 2, of which 2 were waited for; matrix products, arithmetic and copies ran while one was open for 2% of the time, Pallas kernels for 0%

profile of v1, /device:TPU:0, one launch (start us, length us, event | category | flops | bytes accessed | tf_op | source)
XLA Modules:
  0.0 69.5 jit_solution(17653089353550699711)
XLA Ops:
  0.6 0.0 copy-start
  0.6 0.0 copy-start.4
  0.7 0.0 copy-start.5
  0.7 0.0 copy-start.3
  0.7 1.1 %slice.6 = bf16[64,2,8,128]{3,2,1,0:T(8,128)(2,1)S(1)} slice(bf16[512,2,8,128]{3,2,1,0:T(8,128)(2,1)} %param.7), slice={[0:64], [0:2], [0:8], [0:128]} | slice | bytes 524288 | tf_op jit(solution)/shard_map/slice | solution.py:162
  1.8 0.1 constant_dynamic-slice_fusion
  1.9 1.3 %select_reduce_fusion = (s32[]{:T(128)}, pred[8]{0:T(512)(128)(4,1)S(1)}) fusion(s32[8]{0:T(128)} %partner_ref.1, s32[]{:T(128)S(6)} %axis_index.23), kind=kLoop, calls=%fused_computation.6 | loop fusion | flops 23 | bytes 48 | tf_op jit(solution)/shard_map/reduce_sum | solution.py:161
  3.2 0.9 %broadcast_select_fusion.1 = bf16[8,256,128]{2,1,0:T(8,128)(2,1)} fusion(pred[8]{0:T(512)(128)(4,1)S(1)} %get-tuple-element.12, bf16[256,128]{1,0:T(8,128)(2,1)S(1)} %bitcast.17), kind=kLoop, calls=%fused_computation.1 | loop fusion | flops 262144 | bytes 589832 | tf_op jit(solution)/shard_map/jit(_where)/select_n | solution.py:29
  4.1 5.2 %all-to-all-start = ((bf16[8,256,128]{2,1,0:T(8,128)(2,1)}), bf16[8,256,128]{2,1,0:T(8,128)(2,1)S(1)}, u32[]{:S(2)}, u32[]{:S(2)}) async-start(bf16[8,256,128]{2,1,0:T(8,128)(2,1)} %broadcast_select_fusion.1), calls=%async_computation | async-start | bytes 1048576 | tf_op jit(solution)/shard_map/all_to_all | solution.py:164
  9.3 0.0 copy-done.4
  9.3 0.6 dynamic_slice.11
  9.9 0.6 iota_compare_fusion
  10.6 8.5 %all-to-all-done.got_ref = bf16[8,256,128]{2,1,0:T(8,128)(2,1)S(1)} async-done(((bf16[8,256,128]{2,1,0:T(8,128)(2,1)}), bf16[8,256,128]{2,1,0:T(8,128)(2,1)S(1)}, u32[]{:S(2)}, u32[]{:S(2)}) %all-to-all-start) | async-done | bytes 524320 | tf_op jit(solution)/shard_map/all_to_all | solution.py:164
  19.0 0.0 copy-done
  19.0 0.0 copy-done.5
  19.1 0.0 copy-done.3
  19.1 0.0 copy-start.1
  19.1 1.6 %copy-done.1 = bf16[512,16,128]{2,1,0:T(8,128)(2,1)S(1)} copy-done((bf16[512,16,128]{2,1,0:T(8,128)(2,1)S(1)}, bf16[512,16,128]{2,1,0:T(8,128)(2,1)}, u32[]{:S(2)}) %copy-start.1) | copy-done | bytes 2097176
  20.7 0.0 copy-start.2
  20.7 1.6 %copy-done.2 = bf16[512,16,128]{2,1,0:T(8,128)(2,1)S(1)} copy-done((bf16[512,16,128]{2,1,0:T(8,128)(2,1)S(1)}, bf16[512,16,128]{2,1,0:T(8,128)(2,1)}, u32[]{:S(2)}) %copy-start.2) | copy-done | bytes 2097176
  22.2 31.7 %shard_map.85 = (bf16[8192,128]{1,0:T(8,128)(2,1)}, bf16[8192,128]{1,0:T(8,128)(2,1)}, bf16[512,512]{1,0:T(8,128)(2,1)}, bf16[64,512]{1,0:T(8,128)(2,1)S(1)}) custom-call(s32[8]{0:T(128)S(1)} %copy-done.4, s32[8]{0:T(128)S(1)} %copy-done.5, bf16[8192,128]{1,0:T(8,128)(2,1)S(1)} %bitcast.14, bf16[8192,128]{1,0:T(8,128)(2,1)S(1)} %bitcast.15, ...), custom_call_target="tpu_custom_call" | custom-call | tf_op jit(solution)/shard_map/pallas_call | solution.py:171
  53.9 0.9 %broadcast_select_fusion = bf16[8,64,512]{2,1,0:T(8,128)(2,1)} fusion(pred[8]{0:T(512)(128)(4,1)S(1)} %iota_compare_fusion, bf16[64,512]{1,0:T(8,128)(2,1)S(1)} %get-tuple-element.10), kind=kLoop, calls=%fused_computation | loop fusion | flops 262144 | bytes 589832 | tf_op jit(solution)/shard_map/jit(_where)/select_n | solution.py:29
  54.8 3.5 %all-to-all-start.1 = ((bf16[8,64,512]{2,1,0:T(8,128)(2,1)}), bf16[8,64,512]{2,1,0:T(8,128)(2,1)S(1)}, u32[]{:S(2)}, u32[]{:S(2)}) async-start(bf16[8,64,512]{2,1,0:T(8,128)(2,1)} %broadcast_select_fusion), calls=%async_computation.1 | async-start | bytes 1048576 | tf_op jit(solution)/shard_map/all_to_all | solution.py:202
  60.2 7.8 %all-to-all-done.1 = bf16[8,64,512]{2,1,0:T(8,128)(2,1)S(1)} async-done(((bf16[8,64,512]{2,1,0:T(8,128)(2,1)}), bf16[8,64,512]{2,1,0:T(8,128)(2,1)S(1)}, u32[]{:S(2)}, u32[]{:S(2)}) %all-to-all-start.1) | async-done | bytes 524320 | tf_op jit(solution)/shard_map/all_to_all | solution.py:202
  68.0 1.5 %fusion.1 = bf16[512,512]{1,0:T(8,128)(2,1)} fusion(bf16[512,512]{1,0:T(8,128)(2,1)} %get-tuple-element.9, bf16[8,64,512]{2,1,0:T(8,128)(2,1)S(1)} %all-to-all-done.1, s32[]{:T(128)S(6)} %select_n.33), kind=kLoop, calls=%fused_computation.4 | loop fusion | flops 131072 | bytes 196612 | tf_op jit(solution)/shard_map/dynamic_update_slice | solution.py:211
  (1 shorter events, 0.0 us)
Async XLA Ops:
  0.6 18.4 %copy-start = (bf16[512,2,8,128]{3,2,1,0:T(8,128)(2,1)S(1)}, bf16[512,2,8,128]{3,2,1,0:T(8,128)(2,1)}, u32[]{:S(2)}) copy-start(bf16[512,2,8,128]{3,2,1,0:T(8,128)(2,1)} %param.7) | copy-start | bytes 6291460
  0.6 8.7 %copy-start.4 = (s32[8]{0:T(128)S(1)}, s32[8]{0:T(128)}, u32[]{:S(2)}) copy-start(s32[8]{0:T(128)} %partner_ref.1) | copy-start | bytes 100
  0.7 18.4 %copy-start.5 = (s32[8]{0:T(128)S(1)}, s32[8]{0:T(128)}, u32[]{:S(2)}) copy-start(s32[8]{0:T(128)} %blocks_ref.1) | copy-start | bytes 100
  0.7 18.4 %copy-start.3 = (s32[512]{0:T(512)S(1)}, s32[512]{0:T(512)}, u32[]{:S(2)}) copy-start(s32[512]{0:T(512)} %param.9) | copy-start | bytes 6148
  4.1 14.9 %all-to-all-start = ((bf16[8,256,128]{2,1,0:T(8,128)(2,1)}), bf16[8,256,128]{2,1,0:T(8,128)(2,1)S(1)}, u32[]{:S(2)}, u32[]{:S(2)}) async-start(bf16[8,256,128]{2,1,0:T(8,128)(2,1)} %broadcast_select_fusion.1), calls=%async_computation | async-start | bytes 1048576 | tf_op jit(solution)/shard_map/all_to_all | solution.py:164
  19.1 1.6 %copy-start.1 = (bf16[512,16,128]{2,1,0:T(8,128)(2,1)S(1)}, bf16[512,16,128]{2,1,0:T(8,128)(2,1)}, u32[]{:S(2)}) copy-start(bf16[512,16,128]{2,1,0:T(8,128)(2,1)} %param.6) | copy-start | bytes 6291460
  20.7 1.6 %copy-start.2 = (bf16[512,16,128]{2,1,0:T(8,128)(2,1)S(1)}, bf16[512,16,128]{2,1,0:T(8,128)(2,1)}, u32[]{:S(2)}) copy-start(bf16[512,16,128]{2,1,0:T(8,128)(2,1)} %param.8) | copy-start | bytes 6291460
  54.8 13.2 %all-to-all-start.1 = ((bf16[8,64,512]{2,1,0:T(8,128)(2,1)}), bf16[8,64,512]{2,1,0:T(8,128)(2,1)S(1)}, u32[]{:S(2)}, u32[]{:S(2)}) async-start(bf16[8,64,512]{2,1,0:T(8,128)(2,1)} %broadcast_select_fusion), calls=%async_computation.1 | async-start | bytes 1048576 | tf_op jit(solution)/shard_map/all_to_all | solution.py:202

commit v2 on v1

v2 whole, which is shorter than its diff:
```python
import functools
import math

import jax
import jax.numpy as jnp
from jax import lax
from jax.experimental import pallas as pl
from jax.experimental.pallas import tpu as pltpu
from jax.sharding import PartitionSpec as P

HEADS = 64
KVH = 8
PMAX = 64
BLK = 16
ROWS = 128
PAD = 128
MASKED = -1e30
LOG2E = math.log2(math.e)


def from_partner(value, axis, apart):
    mask = 2**apart
    pairs = [(source, source ^ mask) for source in range(lax.axis_size(axis))]
    return lax.ppermute(value, axis, pairs)


def head_total(block, sharing):
    flat = block.reshape(block.shape[0], -1)
    place = lax.axis_index("head")
    for bit in reversed(range(sharing.bit_length() - 1)):
        half = flat.shape[1] // 2
        mine = place // 2**bit % 2
        kept = lax.dynamic_slice_in_dim(flat, mine * half, half, 1)
        given = lax.dynamic_slice_in_dim(flat, (1 - mine) * half, half, 1)
        got = from_partner(given.astype(jnp.bfloat16), "head", bit).astype(given.dtype)
        flat = kept + got
    return flat


def dot(a, b):
    return jnp.dot(a, b, preferred_element_type=jnp.float32)


def dot_t(a, b):
    return lax.dot_general(a, b, (((1,), (1,)), ((), ())), preferred_element_type=jnp.float32)


def attend(
    heads, kvs, per_kv, chunks, peers, merge, scale,
    partner_ref, blocks_ref, q_ref, do_ref, kv_ref, seg_ref,
    out_ref, dq_ref, own_ref, arrived_ref,
    qf, dof, af, dqf, kvf, kcat, vcat, segc, bias, dkt, dvt,
    parcel, got, grads, got_grads, sent, landed, grads_sent, grads_landed,
):
    group, chunk = pl.program_id(0), pl.program_id(1)
    me = lax.axis_index("seq")
    rows = chunks * ROWS
    width = PAD + rows
    piece = ROWS * heads
    last = chunks - 1

    def prompt_copy(d):
        return pltpu.make_async_remote_copy(
            src_ref=parcel,
            dst_ref=got.at[d],
            send_sem=sent.at[d],
            recv_sem=landed.at[d],
            device_id={"seq": lax.rem(me + d + 1, peers + 1)},
            device_id_type=pl.DeviceIdType.MESH,
        )

    def grad_copy(g, d):
        return pltpu.make_async_remote_copy(
            src_ref=grads.at[g],
            dst_ref=got_grads.at[g, d],
            send_sem=grads_sent.at[g, d],
            recv_sem=grads_landed.at[g, d],
            device_id={"seq": lax.rem(me + d + 1, peers + 1)},
            device_id_type=pl.DeviceIdType.MESH,
        )

    def each_peer(act):
        def one(d, carry):
            act(d)
            return carry
        lax.fori_loop(0, peers, one, 0)

    @pl.when((group == 0) & (chunk == 0))
    def _():
        barrier = pltpu.get_barrier_semaphore()
        each_peer(lambda d: pl.semaphore_signal(
            barrier, inc=1, device_id={"seq": lax.rem(me + d + 1, peers + 1)},
            device_id_type=pl.DeviceIdType.MESH,
        ))
        kv_start = lax.axis_index("head") * heads // (HEADS // KVH)
        early = PMAX * 2 * KVH
        kvf[:early, :] = kv_ref[:early, :].astype(jnp.float32)
        for n in range(2 * kvs):
            at = kv_start + n % kvs + n // kvs * KVH
            parcel[n * PMAX:(n + 1) * PMAX, :] = kvf[pl.ds(at, PMAX, stride=2 * KVH), :].astype(jnp.bfloat16)
        pl.semaphore_wait(barrier, peers)
        each_peer(lambda d: prompt_copy(d).start())
        kvf[early:, :] = kv_ref[early:, :].astype(jnp.float32)
        for g in range(kvs):
            k_rows = kvf[pl.ds(kv_start + g, rows, stride=2 * KVH), :]
            v_rows = kvf[pl.ds(kv_start + g + KVH, rows, stride=2 * KVH), :]
            kcat[g, PAD:, :] = k_rows.astype(jnp.bfloat16)
            vcat[g, PAD:, :128] = v_rows.astype(jnp.bfloat16)
            kcat[g, PMAX:PAD, :] = jnp.zeros((PAD - PMAX, 128), jnp.bfloat16)
            vcat[g, PMAX:PAD, :128] = jnp.zeros((PAD - PMAX, 128), jnp.bfloat16)
            vcat[g, :, 128:] = jnp.ones((width, 128), jnp.bfloat16)
        segc[...] = jnp.broadcast_to(seg_ref[...].astype(jnp.float32), (128, rows)).T
        dkt[...] = jnp.zeros_like(dkt)
        dvt[...] = jnp.zeros_like(dvt)

    @pl.when(group == 0)
    def _():
        here = pl.ds(pl.multiple_of(chunk * piece, piece), piece)
        qf[here, :] = q_ref[...].astype(jnp.float32)
        dof[here, :] = do_ref[...].astype(jnp.float32)

    @pl.when((group == 0) & (chunk == 0))
    def _():
        each_peer(lambda d: prompt_copy(d).wait())
        slot = jnp.maximum(lax.rem(me - partner_ref[me] + peers + 1, peers + 1) - 1, 0)
        for g in range(kvs):
            kcat[g, :PMAX, :] = got[slot, g * PMAX:(g + 1) * PMAX, :]
            vcat[g, :PMAX, :128] = got[slot, (kvs + g) * PMAX:(kvs + g + 1) * PMAX, :]

    def work(c):
        wide = PAD + (c + 1) * ROWS
        live = BLK * blocks_ref[partner_ref[me]]
        column = segc[c * ROWS:(c + 1) * ROWS, :]
        place = lax.broadcasted_iota(jnp.int32, (ROWS, 128), 1)
        row = lax.broadcasted_iota(jnp.int32, (ROWS, 128), 0)
        bias[:, :PAD] = jnp.where((column == 1.0) & (place < live), 0.0, MASKED)
        for j in range(c + 1):
            same = column == seg_ref[:, j * ROWS:(j + 1) * ROWS].astype(jnp.float32)
            if j == c:
                same = same & (place <= row)
            bias[:, PAD + j * ROWS:PAD + (j + 1) * ROWS] = jnp.where(same, 0.0, MASKED)

        def spots(i):
            h = group * per_kv + 2 * i + c * piece
            return pl.ds(h, ROWS, stride=heads), pl.ds(h + 1, ROWS, stride=heads)

        def scores(i):
            first, second = spots(i)
            q32 = jnp.concatenate([qf[first, :], qf[second, :]], axis=0)
            q = q32.astype(jnp.bfloat16)
            return q, dot_t(q, kcat[group, :wide, :])

        def softmax(i, q, s):
            first, second = spots(i)
            b = bias[:, :wide]
            t = s * (scale * LOG2E) + jnp.concatenate([b, b], axis=0)
            p = jnp.exp2(t - jnp.max(t, axis=1, keepdims=True))
            pb = p.astype(jnp.bfloat16)
            mixed = dot(pb, vcat[group, :wide, :])
            inverse = 1.0 / mixed[:, 128:]
            attention = (mixed[:, :128] * inverse).astype(jnp.bfloat16).astype(jnp.float32)
            af[first, :] = attention[:ROWS]
            af[second, :] = attention[ROWS:]
            do = jnp.concatenate([dof[first, :], dof[second, :]], axis=0)
            dos = (do * inverse).astype(jnp.bfloat16)
            delta = jnp.sum(dos.astype(jnp.float32) * attention, axis=1, keepdims=True)
            dp = dot_t(dos, vcat[group, :wide, :128])
            ds = (p * (dp - delta)).astype(jnp.bfloat16)
            return q, pb, dos, ds

        def gradients(i, q, pb, dos, ds):
            first, second = spots(i)
            dq = dot(ds, kcat[group, :wide, :]) * scale
            dqf[first, :] = dq[:ROWS]
            dqf[second, :] = dq[ROWS:]
            dkt[group, :, :wide] += dot(q.T, ds)
            dvt[group, :, :wide] += dot(dos.T, pb)

        pairs = per_kv // 2
        scored, soft = {}, {}
        for i in range(pairs + 2):
            if i < pairs:
                scored[i] = scores(i)
            if 0 <= i - 1 < pairs:
                soft[i - 1] = softmax(i - 1, *scored.pop(i - 1))
            if 0 <= i - 2 < pairs:
                gradients(i - 2, *soft.pop(i - 2))

    for c in range(chunks):
        pl.when(chunk == c)(functools.partial(work, c))

    @pl.when(group == kvs - 1)
    def _():
        here = pl.ds(pl.multiple_of(chunk * piece, piece), piece)
        out_ref[...] = af[here, :].astype(jnp.bfloat16)
        dq_ref[...] = dqf[here, :].astype(jnp.bfloat16)

    for g in range(kvs):
        @pl.when((group == g) & (chunk == last))
        def _():
            for part, total in ((0, dkt), (1, dvt)):
                grads[g, :, part * 128:(part + 1) * 128] = (
                    (total[g, :, :PAD] * (1.0 if part else scale)).T[:PMAX].astype(jnp.bfloat16)
                )
            each_peer(lambda d: grad_copy(g, d).start())
            for part, total in ((0, dkt), (1, dvt)):
                at = (2 * g + part) * 128
                own_ref[:, at:at + 128] = (
                    (total[g, :, PAD:] * (1.0 if part else scale)).T.astype(jnp.bfloat16)
                )

    @pl.when((group == kvs - 1) & (chunk == last))
    def _():
        slot = jnp.int32(0)
        for b in range(peers + 1):
            slot = jnp.where(partner_ref[b] == me, lax.rem(me - b + peers + 1, peers + 1) - 1, slot)
        slot = jnp.maximum(slot, 0)
        for g in range(kvs):
            each_peer(lambda d: grad_copy(g, d).wait())
        for g in range(kvs):
            block = got_grads[g, slot]
            at = slice(g * 256, (g + 1) * 256)
            arrived_ref[:, at] = block
            if merge:
                own_ref[:PMAX, at] = (
                    own_ref[:PMAX, at].astype(jnp.float32) + block.astype(jnp.float32)
                ).astype(jnp.bfloat16)


def body(queries, keys_values, grad_out, segments, partner, prompt_blocks):
    rows_here, heads_here, head_dim = queries.shape
    group_size = HEADS // KVH
    kv_here = max(1, heads_here // group_size)
    per_kv = heads_here // kv_here
    sharing = max(1, group_size // heads_here)
    peers = lax.axis_size("seq") - 1
    chunks = rows_here // ROWS
    width = PAD + rows_here
    last = chunks - 1
    block_in = pl.BlockSpec((ROWS * heads_here, head_dim), lambda g, c: (jnp.where(g == 0, c, last), 0))
    block_out = pl.BlockSpec((ROWS * heads_here, head_dim), lambda g, c: (jnp.where(g == kv_here - 1, c, 0), 0))
    whole = pl.BlockSpec(memory_space=pltpu.VMEM)
    flat = jax.ShapeDtypeStruct((rows_here * heads_here, head_dim), jnp.bfloat16)
    f32, bf16 = jnp.float32, jnp.bfloat16
    attention, query_gradient, own, arrived = pl.pallas_call(
        functools.partial(
            attend, heads_here, kv_here, per_kv, chunks, peers, sharing == 1, 1.0 / math.sqrt(head_dim)
        ),
        grid=(kv_here, chunks),
        in_specs=[pl.BlockSpec(memory_space=pltpu.SMEM)] * 2 + [block_in, block_in, whole, whole],
        out_specs=[block_out, block_out, whole, whole],
        out_shape=[
            flat,
            flat,
            jax.ShapeDtypeStruct((rows_here, kv_here * 2 * head_dim), bf16),
            jax.ShapeDtypeStruct((PMAX, kv_here * 2 * head_dim), bf16),
        ],
        scratch_shapes=[pltpu.VMEM((rows_here * heads_here, head_dim), f32)] * 4
        + [
            pltpu.VMEM((rows_here * 2 * KVH, head_dim), f32),
            pltpu.VMEM((kv_here, width, head_dim), bf16),
            pltpu.VMEM((kv_here, width, 2 * head_dim), bf16),
            pltpu.VMEM((rows_here, 128), f32),
            pltpu.VMEM((ROWS, width), f32),
            pltpu.VMEM((kv_here, head_dim, width), f32),
            pltpu.VMEM((kv_here, head_dim, width), f32),
            pltpu.VMEM((2 * kv_here * PMAX, head_dim), bf16),
            pltpu.VMEM((peers, 2 * kv_here * PMAX, head_dim), bf16),
            pltpu.VMEM((kv_here, PMAX, 2 * head_dim), bf16),
            pltpu.VMEM((kv_here, peers, PMAX, 2 * head_dim), bf16),
            pltpu.SemaphoreType.DMA((peers,)),
            pltpu.SemaphoreType.DMA((peers,)),
            pltpu.SemaphoreType.DMA((kv_here, peers)),
            pltpu.SemaphoreType.DMA((kv_here, peers)),
        ],
        compiler_params=pltpu.CompilerParams(
            vmem_limit_bytes=56 * 2**20, collective_id=0, has_side_effects=True
        ),
    )(
        partner,
        prompt_blocks,
        queries.reshape(-1, head_dim),
        grad_out.reshape(-1, head_dim),
        keys_values.reshape(-1, head_dim),
        segments.reshape(1, rows_here),
    )
    if sharing > 1:
        joined = lax.optimization_barrier(jnp.concatenate([own, arrived], axis=0))
        summed = head_total(joined.astype(jnp.float32), sharing)
        own, arrived = summed[:rows_here], summed[rows_here:].astype(jnp.bfloat16)
        head_rows = own[:PMAX] + arrived.astype(jnp.float32)
        own = jnp.concatenate([head_rows, own[PMAX:]], axis=0).astype(jnp.bfloat16)
    return (attention.reshape(queries.shape), query_gradient.reshape(queries.shape), own)


def solution(mesh):
    in_specs = (
        P("seq", "head", None),
        P("seq", None, None, None),
        P("seq", "head", None),
        P("seq"),
        P(),
        P(),
    )
    out_specs = (P("seq", "head", None), P("seq", "head", None), P("seq", "head"))
    return jax.shard_map(body, mesh=mesh, in_specs=in_specs, out_specs=out_specs, check_vma=False)
```

time: 69.9 us -> 45.7 us (0.65)
  waiting for transfers between devices: 16.3 us -> 0 us
  starting transfers between devices: 8.66 us -> 0 us
  Pallas kernels: 31.7 us -> 39.2 us
  other arithmetic: 5.26 us -> 0 us
  between operations: 2.65 us -> 0.65 us
    all_to_all x2 -> x0, waiting for transfers between devices: 16.3 us -> none  [the longest x1 8.49 us: body(): lax.all_to_all(slotted(parcel, partner == self_index), 'seq', split_axis=...]
    all_to_all x2 -> x0, starting transfers between devices: 8.66 us -> none  [the longest x1 5.17 us: body(): lax.all_to_all(slotted(parcel, partner == self_index), 'seq', split_axis=...]
    pallas_call x1, Pallas kernels: 31.7 us -> 39.2 us  [body(): pl.pallas_call(functools.partial(attend, heads_here, kv_here, per_kv, chu...]
    unnamed x13 -> x7, local copies, waits for them, and re-layouts: 3.21 us -> 5.61 us
    select_n x2 -> x0, other arithmetic: 1.8 us -> none  [slotted(): return jnp.where(mask, parcel[None], jnp.zeros((), parcel.dtype))]
    dynamic_update_slice x1 -> x0, other arithmetic: 1.49 us -> none  [body(): lax.dynamic_update_slice(own.astype(jnp.bfloat16), head_rows.astype(jnp.b...]
    reduce_sum x1 -> x0, other arithmetic: 1.32 us -> none  [body(): source = jnp.sum(jnp.where(partner == self_index, bin_ids, 0))]
    slice x1 -> x0, local copies, waits for them, and re-layouts: 1.11 us -> none  [body(): prompt = lax.dynamic_slice_in_dim(keys_values[:PMAX], kv_start, kv_here, 2)]
  transfers between devices with their start and end apart: 2 -> 0, of which waited for: 2 -> 0; matrix products, arithmetic and copies ran while one was open for 2% -> 0% of each run, Pallas kernels for 0% -> 0%
where the time goes in v2:
time: 45.7 us; the launch traced here: 45.5 us
  Pallas kernels  39.2 us (86%)
  local copies, waits for them, and re-layouts  5.61 us (12%)
  between operations  0.65 us (1%)
    pallas_call x1, Pallas kernels, body(): pl.pallas_call(functools.partial(attend, heads_here, kv_here, per_kv, chu...  39.2 us
    unnamed x7, local copies, waits for them, and re-layouts  5.61 us

profile of v2, /device:TPU:0, one launch (start us, length us, event | category | flops | bytes accessed | tf_op | source)
XLA Modules:
  0.0 45.5 jit_solution(2226834297022716029)
XLA Ops:
  0.6 39.2 %shard_map.85 = (bf16[8192,128]{1,0:T(8,128)(2,1)}, bf16[8192,128]{1,0:T(8,128)(2,1)}, bf16[512,512]{1,0:T(8,128)(2,1)}, bf16[64,512]{1,0:T(8,128)(2,1)}) custom-call(s32[8]{0:T(128)} %partner_ref.1, s32[8]{0:T(128)} %blocks_ref.1, bf16[8192,128]{1,0:T(8,128)(2,1)} %bitcast.6, bf16[8192,128]{1,0:T(8,128)(2,1)} %bitcast.7, bf16[8192,128]{1,0:T(8,128)(2,1)} %bitcast.8, ...), custom_call_target="tpu_custom_call" | custom-call | tf_op jit(solution)/shard_map/pallas_call | solution.py:245
  39.8 0.0 copy-start
  39.9 3.4 %copy.12 = bf16[512,16,128]{2,1,0:T(8,128)(2,1)} copy(bf16[512,16,128]{2,1,0:T(8,128)(2,1)} %bitcast.10) | data formatting | bytes 4194304
  43.3 0.0 copy-done
  43.3 0.0 copy-start.1
  43.3 1.3 %copy.13 = bf16[512,16,128]{2,1,0:T(8,128)(2,1)} copy(bf16[512,16,128]{2,1,0:T(8,128)(2,1)S(1)} %bitcast.9) | data formatting | bytes 4194304
  44.6 0.1 copy-done.1
  44.7 0.8 %copy.14 = bf16[512,512]{1,0:T(8,128)(2,1)} copy(bf16[512,512]{1,0:T(8,128)(2,1)S(1)} %copy-done.1) | data formatting | bytes 1048576
Async XLA Ops:
  39.8 3.4 %copy-start = (bf16[8192,128]{1,0:T(8,128)(2,1)S(1)}, bf16[8192,128]{1,0:T(8,128)(2,1)}, u32[]{:S(2)}) copy-start(bf16[8192,128]{1,0:T(8,128)(2,1)} %get-tuple-element.7) | copy-start | bytes 6291460
  43.3 1.4 %copy-start.1 = (bf16[512,512]{1,0:T(8,128)(2,1)S(1)}, bf16[512,512]{1,0:T(8,128)(2,1)}, u32[]{:S(2)}) copy-start(bf16[512,512]{1,0:T(8,128)(2,1)} %get-tuple-element.14) | copy-start | bytes 1572868

commit v3 on v2

v3 whole, which is shorter than its diff:
```python
import functools
import math

import jax
import jax.numpy as jnp
from jax import lax
from jax.experimental import pallas as pl
from jax.experimental.pallas import tpu as pltpu
from jax.sharding import PartitionSpec as P

HEADS = 64
KVH = 8
PMAX = 64
BLK = 16
ROWS = 128
PAD = 128
MASKED = -1e30
LOG2E = math.log2(math.e)


def from_partner(value, axis, apart):
    mask = 2**apart
    pairs = [(source, source ^ mask) for source in range(lax.axis_size(axis))]
    return lax.ppermute(value, axis, pairs)


def head_total(block, sharing):
    flat = block.reshape(block.shape[0], -1)
    place = lax.axis_index("head")
    for bit in reversed(range(sharing.bit_length() - 1)):
        half = flat.shape[1] // 2
        mine = place // 2**bit % 2
        kept = lax.dynamic_slice_in_dim(flat, mine * half, half, 1)
        given = lax.dynamic_slice_in_dim(flat, (1 - mine) * half, half, 1)
        got = from_partner(given.astype(jnp.bfloat16), "head", bit).astype(given.dtype)
        flat = kept + got
    return flat


def dot(a, b):
    return jnp.dot(a, b, preferred_element_type=jnp.float32)


def dot_t(a, b):
    return lax.dot_general(a, b, (((1,), (1,)), ((), ())), preferred_element_type=jnp.float32)


def attend(
    heads, kvs, per_kv, chunks, peers, merge, scale,
    partner_ref, blocks_ref, q_hbm, do_hbm, kv_hbm, seg_ref,
    out_ref, dq_ref, own_ref, arrived_ref,
    q_ref, do_ref, kv_ref,
    qf, dof, dqf, af, kcat, vcat, segc, bias, dkt, dvt,
    early_s, early_dp, kept_pb, kept_ds, kept_dos,
    parcel, got, grads, got_grads, sent, landed, grads_sent, grads_landed, kv_sem, q_sem, do_sem,
):
    me = lax.axis_index("seq")
    kvf = af
    rows = chunks * ROWS
    width = PAD + rows
    piece = ROWS * heads
    last = chunks - 1

    def prompt_copy(d):
        return pltpu.make_async_remote_copy(
            src_ref=parcel,
            dst_ref=got.at[d],
            send_sem=sent.at[d],
            recv_sem=landed.at[d],
            device_id={"seq": lax.rem(me + d + 1, peers + 1)},
            device_id_type=pl.DeviceIdType.MESH,
        )

    def grad_copy(g, d):
        return pltpu.make_async_remote_copy(
            src_ref=grads.at[g],
            dst_ref=got_grads.at[g, d],
            send_sem=grads_sent.at[g, d],
            recv_sem=grads_landed.at[g, d],
            device_id={"seq": lax.rem(me + d + 1, peers + 1)},
            device_id_type=pl.DeviceIdType.MESH,
        )

    def each_peer(act):
        def one(d, carry):
            act(d)
            return carry
        lax.fori_loop(0, peers, one, 0)

    def separately(act):
        pl.when(me >= 0)(act)

    def span(c):
        return pl.ds(c * piece, piece)

    early = PMAX * 2 * KVH
    loads = [
        pltpu.make_async_copy(kv_hbm.at[pl.ds(0, early)], kv_ref.at[pl.ds(0, early)], kv_sem.at[0]),
        pltpu.make_async_copy(
            kv_hbm.at[pl.ds(early, rows * 2 * KVH - early)],
            kv_ref.at[pl.ds(early, rows * 2 * KVH - early)],
            kv_sem.at[1],
        ),
    ]
    q_loads = [pltpu.make_async_copy(q_hbm.at[span(c)], q_ref.at[span(c)], q_sem.at[c]) for c in range(chunks)]
    do_loads = [pltpu.make_async_copy(do_hbm.at[span(c)], do_ref.at[span(c)], do_sem.at[c]) for c in range(chunks)]
    for load in loads + q_loads + do_loads:
        load.start()
    barrier = pltpu.get_barrier_semaphore()
    each_peer(lambda d: pl.semaphore_signal(
        barrier, inc=1, device_id={"seq": lax.rem(me + d + 1, peers + 1)},
        device_id_type=pl.DeviceIdType.MESH,
    ))
    kv_start = lax.axis_index("head") * heads // (HEADS // KVH)
    loads[0].wait()
    kvf[:early, :] = kv_ref[:early, :].astype(jnp.float32)
    for n in range(2 * kvs):
        at = kv_start + n % kvs + n // kvs * KVH
        parcel[n * PMAX:(n + 1) * PMAX, :] = kvf[pl.ds(at, PMAX, stride=2 * KVH), :].astype(jnp.bfloat16)
    pl.semaphore_wait(barrier, peers)
    each_peer(lambda d: prompt_copy(d).start())
    loads[1].wait()
    kvf[early:, :] = kv_ref[early:, :].astype(jnp.float32)
    for g in range(kvs):
        k_rows = kvf[pl.ds(kv_start + g, rows, stride=2 * KVH), :]
        v_rows = kvf[pl.ds(kv_start + g + KVH, rows, stride=2 * KVH), :]
        kcat[g, PAD:, :] = k_rows.astype(jnp.bfloat16)
        vcat[g, PAD:, :128] = v_rows.astype(jnp.bfloat16)
        kcat[g, PMAX:PAD, :] = jnp.zeros((PAD - PMAX, 128), jnp.bfloat16)
        vcat[g, PMAX:PAD, :128] = jnp.zeros((PAD - PMAX, 128), jnp.bfloat16)
        vcat[g, :, 128:] = jnp.ones((width, 128), jnp.bfloat16)
    segc[...] = jnp.broadcast_to(seg_ref[...].astype(jnp.float32), (128, rows)).T
    dkt[...] = jnp.zeros_like(dkt)
    dvt[...] = jnp.zeros_like(dvt)

    pairs = per_kv // 2

    def spots(g, c, i):
        h = g * per_kv + 2 * i + c * piece
        return pl.ds(h, ROWS, stride=heads), pl.ds(h + 1, ROWS, stride=heads)

    def both(ref, g, c, i):
        first, second = spots(g, c, i)
        return jnp.concatenate([ref[first, :], ref[second, :]], axis=0)

    def prepare(c):
        q_loads[c].wait()
        do_loads[c].wait()
        qf[span(c), :] = q_ref[span(c), :].astype(jnp.float32)
        dof[span(c), :] = do_ref[span(c), :].astype(jnp.float32)
        size = (c + 1) * ROWS
        start = c * (c + 1) // 2 * ROWS
        for i in range(pairs):
            q = both(qf, 0, c, i).astype(jnp.bfloat16)
            do = both(dof, 0, c, i).astype(jnp.bfloat16)
            early_s[i, :, start:start + size] = dot_t(q, kcat[0, PAD:PAD + size, :])
            early_dp[i, :, start:start + size] = dot_t(do, vcat[0, PAD:PAD + size, :128])

    for c in range(chunks):
        separately(functools.partial(prepare, c))

    each_peer(lambda d: prompt_copy(d).wait())
    slot = jnp.maximum(lax.rem(me - partner_ref[me] + peers + 1, peers + 1) - 1, 0)
    for g in range(kvs):
        kcat[g, :PMAX, :] = got[slot, g * PMAX:(g + 1) * PMAX, :]
        vcat[g, :PMAX, :128] = got[slot, (kvs + g) * PMAX:(kvs + g + 1) * PMAX, :]

    def work(g, c):
        wide = PAD + (c + 1) * ROWS
        size = (c + 1) * ROWS
        start = c * (c + 1) // 2 * ROWS
        final = g == kvs - 1 and c == last
        live = BLK * blocks_ref[partner_ref[me]]
        column = segc[c * ROWS:(c + 1) * ROWS, :]
        place = lax.broadcasted_iota(jnp.int32, (ROWS, 128), 1)
        row = lax.broadcasted_iota(jnp.int32, (ROWS, 128), 0)
        bias[:, :PAD] = jnp.where((column == 1.0) & (place < live), 0.0, MASKED)
        for j in range(c + 1):
            same = column == seg_ref[:, j * ROWS:(j + 1) * ROWS].astype(jnp.float32)
            if j == c:
                same = same & (place <= row)
            bias[:, PAD + j * ROWS:PAD + (j + 1) * ROWS] = jnp.where(same, 0.0, MASKED)

        def scores(i):
            q = both(qf, g, c, i).astype(jnp.bfloat16)
            do = both(dof, g, c, i)
            low = do.astype(jnp.bfloat16)
            if g == 0:
                s = jnp.concatenate([dot_t(q, kcat[g, :PAD, :]), early_s[i, :, start:start + size]], axis=1)
                dp = jnp.concatenate([dot_t(low, vcat[g, :PAD, :128]), early_dp[i, :, start:start + size]], axis=1)
            else:
                s = dot_t(q, kcat[g, :wide, :])
                dp = dot_t(low, vcat[g, :wide, :128])
            return q, do, s, dp

        def softmax(i, q, do, s, dp):
            first, second = spots(g, c, i)
            b = bias[:, :wide]
            t = s * (scale * LOG2E) + jnp.concatenate([b, b], axis=0)
            p = jnp.exp2(t - jnp.max(t, axis=1, keepdims=True))
            pb = p.astype(jnp.bfloat16)
            mixed = dot(pb, vcat[g, :wide, :])
            inverse = 1.0 / mixed[:, 128:]
            attention = (mixed[:, :128] * inverse).astype(jnp.bfloat16).astype(jnp.float32)
            af[first, :] = attention[:ROWS]
            af[second, :] = attention[ROWS:]
            dos = (do * inverse).astype(jnp.bfloat16)
            delta = jnp.sum(do * attention, axis=1, keepdims=True)
            ds = (p * inverse[:, :1] * (dp - delta)).astype(jnp.bfloat16)
            return q, pb, dos, ds

        def query_part(i, ds):
            first, second = spots(g, c, i)
            dq = dot(ds, kcat[g, :wide, :]) * scale
            dqf[first, :] = dq[:ROWS]
            dqf[second, :] = dq[ROWS:]

        def gradients(i, q, pb, dos, ds):
            if final:
                kept_pb[i], kept_ds[i], kept_dos[i] = pb, ds, dos
                dkt[g, :, :PAD] += dot(q.T, ds[:, :PAD])
                dvt[g, :, :PAD] += dot(dos.T, pb[:, :PAD])
            else:
                query_part(i, ds)
                dkt[g, :, :wide] += dot(q.T, ds)
                dvt[g, :, :wide] += dot(dos.T, pb)

        scored, soft = {}, {}
        for i in range(pairs + 2):
            if i < pairs:
                scored[i] = scores(i)
            if 0 <= i - 1 < pairs:
                soft[i - 1] = softmax(i - 1, *scored.pop(i - 1))
            if 0 <= i - 2 < pairs:
                gradients(i - 2, *soft.pop(i - 2))
        if c == last:
            for part, total in ((0, dkt), (1, dvt)):
                grads[g, :, part * 128:(part + 1) * 128] = (
                    (total[g, :, :PAD] * (1.0 if part else scale)).T[:PMAX].astype(jnp.bfloat16)
                )
            each_peer(lambda d: grad_copy(g, d).start())
        if final:
            for i in range(pairs):
                q = both(qf, g, c, i).astype(jnp.bfloat16)
                ds, pb, dos = kept_ds[i], kept_pb[i], kept_dos[i]
                query_part(i, ds)
                dkt[g, :, PAD:] += dot(q.T, ds[:, PAD:])
                dvt[g, :, PAD:] += dot(dos.T, pb[:, PAD:])
        if c == last:
            for part, total in ((0, dkt), (1, dvt)):
                at = (2 * g + part) * 128
                own_ref[:, at:at + 128] = (
                    (total[g, :, PAD:] * (1.0 if part else scale)).T.astype(jnp.bfloat16)
                )
        if g == kvs - 1:
            out_ref[span(c), :] = af[span(c), :].astype(jnp.bfloat16)
            dq_ref[span(c), :] = dqf[span(c), :].astype(jnp.bfloat16)

    for g in range(kvs):
        for c in range(chunks):
            separately(functools.partial(work, g, c))

    slot = jnp.int32(0)
    for b in range(peers + 1):
        slot = jnp.where(partner_ref[b] == me, lax.rem(me - b + peers + 1, peers + 1) - 1, slot)
    slot = jnp.maximum(slot, 0)
    for g in range(kvs):
        each_peer(lambda d: grad_copy(g, d).wait())
    for g in range(kvs):
        block = got_grads[g, slot]
        at = slice(g * 256, (g + 1) * 256)
        arrived_ref[:, at] = block
        if merge:
            own_ref[:PMAX, at] = (
                own_ref[:PMAX, at].astype(jnp.float32) + block.astype(jnp.float32)
            ).astype(jnp.bfloat16)


def body(queries, keys_values, grad_out, segments, partner, prompt_blocks):
    rows_here, heads_here, head_dim = queries.shape
    group_size = HEADS // KVH
    kv_here = max(1, heads_here // group_size)
    per_kv = heads_here // kv_here
    sharing = max(1, group_size // heads_here)
    peers = lax.axis_size("seq") - 1
    chunks = rows_here // ROWS
    width = PAD + rows_here
    pairs = per_kv // 2
    far = pl.BlockSpec(memory_space=pl.ANY)
    whole = pl.BlockSpec(memory_space=pltpu.VMEM)
    flat = jax.ShapeDtypeStruct((rows_here * heads_here, head_dim), jnp.bfloat16)
    f32, bf16 = jnp.float32, jnp.bfloat16
    attention, query_gradient, own, arrived = pl.pallas_call(
        functools.partial(
            attend, heads_here, kv_here, per_kv, chunks, peers, sharing == 1, 1.0 / math.sqrt(head_dim)
        ),
        in_specs=[pl.BlockSpec(memory_space=pltpu.SMEM)] * 2 + [far, far, far, whole],
        out_specs=[whole] * 4,
        out_shape=[
            flat,
            flat,
            jax.ShapeDtypeStruct((rows_here, kv_here * 2 * head_dim), bf16),
            jax.ShapeDtypeStruct((PMAX, kv_here * 2 * head_dim), bf16),
        ],
        scratch_shapes=[pltpu.VMEM((rows_here * heads_here, head_dim), bf16)] * 2
        + [pltpu.VMEM((rows_here * 2 * KVH, head_dim), bf16)]
        + [pltpu.VMEM((rows_here * heads_here, head_dim), f32)] * 3
        + [
            pltpu.VMEM((rows_here * max(heads_here, 2 * KVH), head_dim), f32),
            pltpu.VMEM((kv_here, width, head_dim), bf16),
            pltpu.VMEM((kv_here, width, 2 * head_dim), bf16),
            pltpu.VMEM((rows_here, 128), f32),
            pltpu.VMEM((ROWS, width), f32),
            pltpu.VMEM((kv_here, head_dim, width), f32),
            pltpu.VMEM((kv_here, head_dim, width), f32),
            pltpu.VMEM((pairs, 2 * ROWS, chunks * (chunks + 1) // 2 * ROWS), f32),
            pltpu.VMEM((pairs, 2 * ROWS, chunks * (chunks + 1) // 2 * ROWS), f32),
            pltpu.VMEM((pairs, 2 * ROWS, width), bf16),
            pltpu.VMEM((pairs, 2 * ROWS, width), bf16),
            pltpu.VMEM((pairs, 2 * ROWS, head_dim), bf16),
            pltpu.VMEM((2 * kv_here * PMAX, head_dim), bf16),
            pltpu.VMEM((peers, 2 * kv_here * PMAX, head_dim), bf16),
            pltpu.VMEM((kv_here, PMAX, 2 * head_dim), bf16),
            pltpu.VMEM((kv_here, peers, PMAX, 2 * head_dim), bf16),
            pltpu.SemaphoreType.DMA((peers,)),
            pltpu.SemaphoreType.DMA((peers,)),
            pltpu.SemaphoreType.DMA((kv_here, peers)),
            pltpu.SemaphoreType.DMA((kv_here, peers)),
            pltpu.SemaphoreType.DMA((2,)),
            pltpu.SemaphoreType.DMA((chunks,)),
            pltpu.SemaphoreType.DMA((chunks,)),
        ],
        compiler_params=pltpu.CompilerParams(
            vmem_limit_bytes=48 * 2**20, collective_id=0, has_side_effects=True
        ),
    )(
        partner,
        prompt_blocks,
        queries.reshape(-1, head_dim),
        grad_out.reshape(-1, head_dim),
        keys_values.reshape(-1, head_dim),
        segments.reshape(1, rows_here),
    )
    if sharing > 1:
        joined = lax.optimization_barrier(jnp.concatenate([own, arrived], axis=0))
        summed = head_total(joined.astype(jnp.float32), sharing)
        own, arrived = summed[:rows_here], summed[rows_here:].astype(jnp.bfloat16)
        head_rows = own[:PMAX] + arrived.astype(jnp.float32)
        own = jnp.concatenate([head_rows, own[PMAX:]], axis=0).astype(jnp.bfloat16)
    return (attention.reshape(queries.shape), query_gradient.reshape(queries.shape), own)


def solution(mesh):
    in_specs = (
        P("seq", "head", None),
        P("seq", None, None, None),
        P("seq", "head", None),
        P("seq"),
        P(),
        P(),
    )
    out_specs = (P("seq", "head", None), P("seq", "head", None), P("seq", "head"))
    return jax.shard_map(body, mesh=mesh, in_specs=in_specs, out_specs=out_specs, check_vma=False)
```

time: 45.7 us -> 41.4 us (0.906)
  Pallas kernels: 39.2 us -> 35.1 us
    pallas_call x1, Pallas kernels: 39.2 us -> 35.1 us  [body(): pl.pallas_call(functools.partial(attend, heads_here, kv_here, per_kv, chu...]
    unnamed x7 -> x9, local copies, waits for them, and re-layouts: 5.61 us -> 5.42 us
where the time goes in v3:
time: 41.4 us; the launch traced here: 41.2 us
  Pallas kernels  35.1 us (85%)
  local copies, waits for them, and re-layouts  5.42 us (13%)
  between operations  0.65 us (2%)
    pallas_call x1, Pallas kernels, body(): pl.pallas_call(functools.partial(attend, heads_here, kv_here, per_kv, chu...  35.1 us
    unnamed x9, local copies, waits for them, and re-layouts  5.42 us

profile of v3, /device:TPU:0, one launch (start us, length us, event | category | flops | bytes accessed | tf_op | source)
XLA Modules:
  0.0 41.2 jit_solution(15342648841397418373)
XLA Ops:
  0.6 0.0 copy-start
  0.6 0.7 %copy-done = s32[512]{0:T(512)S(1)} copy-done((s32[512]{0:T(512)S(1)}, s32[512]{0:T(512)}, u32[]{:S(2)}) %copy-start) | copy-done | bytes 2072
  1.3 0.0 copy-start.1
  1.3 0.7 %copy-done.1 = s32[8]{0:T(128)S(1)} copy-done((s32[8]{0:T(128)S(1)}, s32[8]{0:T(128)}, u32[]{:S(2)}) %copy-start.1) | copy-done | bytes 56
  2.0 0.0 copy-start.2
  2.0 0.7 %copy-done.2 = s32[8]{0:T(128)S(1)} copy-done((s32[8]{0:T(128)S(1)}, s32[8]{0:T(128)}, u32[]{:S(2)}) %copy-start.2) | copy-done | bytes 56
  2.6 35.1 %shard_map.85 = (bf16[8192,128]{1,0:T(8,128)(2,1)S(1)}, bf16[8192,128]{1,0:T(8,128)(2,1)S(1)}, bf16[512,512]{1,0:T(8,128)(2,1)S(1)}, bf16[64,512]{1,0:T(8,128)(2,1)}) custom-call(s32[8]{0:T(128)S(1)} %copy-done.1, s32[8]{0:T(128)S(1)} %copy-done.2, bf16[8192,128]{1,0:T(8,128)(2,1)} %bitcast.9, bf16[8192,128]{1,0:T(8,128)(2,1)} %bitcast.10, ...), custom_call_target="tpu_custom_call" | custom-call | tf_op jit(solution)/shard_map/pallas_call | solution.py:293
  37.8 1.3 %copy.12 = bf16[512,16,128]{2,1,0:T(8,128)(2,1)} copy(bf16[512,16,128]{2,1,0:T(8,128)(2,1)S(1)} %bitcast.7) | data formatting | bytes 4194304
  39.1 1.3 %copy.13 = bf16[512,16,128]{2,1,0:T(8,128)(2,1)} copy(bf16[512,16,128]{2,1,0:T(8,128)(2,1)S(1)} %bitcast.6) | data formatting | bytes 4194304
  40.4 0.8 %copy.14 = bf16[512,512]{1,0:T(8,128)(2,1)} copy(bf16[512,512]{1,0:T(8,128)(2,1)S(1)} %get-tuple-element.14) | data formatting | bytes 1048576
Async XLA Ops:
  0.6 0.7 %copy-start = (s32[512]{0:T(512)S(1)}, s32[512]{0:T(512)}, u32[]{:S(2)}) copy-start(s32[512]{0:T(512)} %param.9) | copy-start | bytes 6148
  1.3 0.7 %copy-start.1 = (s32[8]{0:T(128)S(1)}, s32[8]{0:T(128)}, u32[]{:S(2)}) copy-start(s32[8]{0:T(128)} %partner_ref.1) | copy-start | bytes 100
  2.0 0.7 %copy-start.2 = (s32[8]{0:T(128)S(1)}, s32[8]{0:T(128)}, u32[]{:S(2)}) copy-start(s32[8]{0:T(128)} %blocks_ref.1) | copy-start | bytes 100

commit v4 on v3

--- a/solution.py
+++ b/solution.py
@@ -14,6 +14,7 @@
 BLK = 16
 ROWS = 128
 PAD = 128
+TILE = 32
 MASKED = -1e30
 LOG2E = math.log2(math.e)
 
@@ -195,19 +196,26 @@
 
         def softmax(i, q, do, s, dp):
             first, second = spots(g, c, i)
-            b = bias[:, :wide]
-            t = s * (scale * LOG2E) + jnp.concatenate([b, b], axis=0)
-            p = jnp.exp2(t - jnp.max(t, axis=1, keepdims=True))
-            pb = p.astype(jnp.bfloat16)
+            tiles = [slice(r, r + TILE) for r in range(0, 2 * ROWS, TILE)]
+            low = []
+            for tile in tiles:
+                row = tile.start % ROWS
+                t = s[tile] * (scale * LOG2E) + bias[row:row + TILE, :wide]
+                low.append(jnp.exp2(t - jnp.max(t, axis=1, keepdims=True)).astype(jnp.bfloat16))
+            pb = jnp.concatenate(low, axis=0)
             mixed = dot(pb, vcat[g, :wide, :])
-            inverse = 1.0 / mixed[:, 128:]
-            attention = (mixed[:, :128] * inverse).astype(jnp.bfloat16).astype(jnp.float32)
+            outs, doss, dss = [], [], []
+            for tile, p in zip(tiles, low):
+                inverse = 1.0 / mixed[tile, 128:]
+                attention = (mixed[tile, :128] * inverse).astype(jnp.bfloat16).astype(jnp.float32)
+                outs.append(attention)
+                doss.append((do[tile] * inverse).astype(jnp.bfloat16))
+                delta = jnp.sum(do[tile] * attention, axis=1, keepdims=True)
+                dss.append(p * ((dp[tile] - delta) * inverse[:, :1]).astype(jnp.bfloat16))
+            attention = jnp.concatenate(outs, axis=0)
             af[first, :] = attention[:ROWS]
             af[second, :] = attention[ROWS:]
-            dos = (do * inverse).astype(jnp.bfloat16)
-            delta = jnp.sum(do * attention, axis=1, keepdims=True)
-            ds = (p * inverse[:, :1] * (dp - delta)).astype(jnp.bfloat16)
-            return q, pb, dos, ds
+            return q, pb, jnp.concatenate(doss, axis=0), jnp.concatenate(dss, axis=0)
 
         def query_part(i, ds):
             first, second = spots(g, c, i)

time: 41.4 us -> 40.9 us (0.988)
  Pallas kernels: 35.1 us -> 34.6 us
    pallas_call x1, Pallas kernels: 35.1 us -> 34.6 us  [body(): pl.pallas_call(functools.partial(attend, heads_here, kv_here, per_kv, chu...]
where the time goes in v4:
time: 40.9 us; the launch traced here: 40.6 us
  Pallas kernels  34.6 us (85%)
  local copies, waits for them, and re-layouts  5.42 us (13%)
  between operations  0.65 us (2%)
    pallas_call x1, Pallas kernels, body(): pl.pallas_call(functools.partial(attend, heads_here, kv_here, per_kv, chu...  34.6 us
    unnamed x9, local copies, waits for them, and re-layouts  5.42 us

profile of v4, /device:TPU:0, one launch (start us, length us, event | category | flops | bytes accessed | tf_op | source)
XLA Modules:
  0.0 40.6 jit_solution(10963342793703818038)
XLA Ops:
  0.6 0.0 copy-start
  0.6 0.7 %copy-done = s32[512]{0:T(512)S(1)} copy-done((s32[512]{0:T(512)S(1)}, s32[512]{0:T(512)}, u32[]{:S(2)}) %copy-start) | copy-done | bytes 2072
  1.3 0.0 copy-start.1
  1.3 0.7 %copy-done.1 = s32[8]{0:T(128)S(1)} copy-done((s32[8]{0:T(128)S(1)}, s32[8]{0:T(128)}, u32[]{:S(2)}) %copy-start.1) | copy-done | bytes 56
  2.0 0.0 copy-start.2
  2.0 0.7 %copy-done.2 = s32[8]{0:T(128)S(1)} copy-done((s32[8]{0:T(128)S(1)}, s32[8]{0:T(128)}, u32[]{:S(2)}) %copy-start.2) | copy-done | bytes 56
  2.6 34.6 %shard_map.85 = (bf16[8192,128]{1,0:T(8,128)(2,1)S(1)}, bf16[8192,128]{1,0:T(8,128)(2,1)S(1)}, bf16[512,512]{1,0:T(8,128)(2,1)S(1)}, bf16[64,512]{1,0:T(8,128)(2,1)}) custom-call(s32[8]{0:T(128)S(1)} %copy-done.1, s32[8]{0:T(128)S(1)} %copy-done.2, bf16[8192,128]{1,0:T(8,128)(2,1)} %bitcast.9, bf16[8192,128]{1,0:T(8,128)(2,1)} %bitcast.10, ...), custom_call_target="tpu_custom_call" | custom-call | tf_op jit(solution)/shard_map/pallas_call | solution.py:301
  37.2 1.3 %copy.12 = bf16[512,16,128]{2,1,0:T(8,128)(2,1)} copy(bf16[512,16,128]{2,1,0:T(8,128)(2,1)S(1)} %bitcast.7) | data formatting | bytes 4194304
  38.5 1.3 %copy.13 = bf16[512,16,128]{2,1,0:T(8,128)(2,1)} copy(bf16[512,16,128]{2,1,0:T(8,128)(2,1)S(1)} %bitcast.6) | data formatting | bytes 4194304
  39.9 0.8 %copy.14 = bf16[512,512]{1,0:T(8,128)(2,1)} copy(bf16[512,512]{1,0:T(8,128)(2,1)S(1)} %get-tuple-element.14) | data formatting | bytes 1048576
Async XLA Ops:
  0.6 0.7 %copy-start = (s32[512]{0:T(512)S(1)}, s32[512]{0:T(512)}, u32[]{:S(2)}) copy-start(s32[512]{0:T(512)} %param.9) | copy-start | bytes 6148
  1.3 0.7 %copy-start.1 = (s32[8]{0:T(128)S(1)}, s32[8]{0:T(128)}, u32[]{:S(2)}) copy-start(s32[8]{0:T(128)} %partner_ref.1) | copy-start | bytes 100
  2.0 0.7 %copy-start.2 = (s32[8]{0:T(128)S(1)}, s32[8]{0:T(128)}, u32[]{:S(2)}) copy-start(s32[8]{0:T(128)} %blocks_ref.1) | copy-start | bytes 100

commit v5 on v4

--- a/solution.py
+++ b/solution.py
@@ -15,6 +15,7 @@
 ROWS = 128
 PAD = 128
 TILE = 32
+TOGETHER = 4
 MASKED = -1e30
 LOG2E = math.log2(math.e)
 
@@ -134,15 +135,14 @@
     dkt[...] = jnp.zeros_like(dkt)
     dvt[...] = jnp.zeros_like(dvt)
 
-    pairs = per_kv // 2
+    pairs = per_kv // TOGETHER
 
     def spots(g, c, i):
-        h = g * per_kv + 2 * i + c * piece
-        return pl.ds(h, ROWS, stride=heads), pl.ds(h + 1, ROWS, stride=heads)
+        h = g * per_kv + TOGETHER * i + c * piece
+        return [pl.ds(h + n, ROWS, stride=heads) for n in range(TOGETHER)]
 
     def both(ref, g, c, i):
-        first, second = spots(g, c, i)
-        return jnp.concatenate([ref[first, :], ref[second, :]], axis=0)
+        return jnp.concatenate([ref[spot, :] for spot in spots(g, c, i)], axis=0)
 
     def prepare(c):
         q_loads[c].wait()
@@ -195,8 +195,7 @@
             return q, do, s, dp
 
         def softmax(i, q, do, s, dp):
-            first, second = spots(g, c, i)
-            tiles = [slice(r, r + TILE) for r in range(0, 2 * ROWS, TILE)]
+            tiles = [slice(r, r + TILE) for r in range(0, TOGETHER * ROWS, TILE)]
             low = []
             for tile in tiles:
                 row = tile.start % ROWS
@@ -213,15 +212,14 @@
                 delta = jnp.sum(do[tile] * attention, axis=1, keepdims=True)
                 dss.append(p * ((dp[tile] - delta) * inverse[:, :1]).astype(jnp.bfloat16))
             attention = jnp.concatenate(outs, axis=0)
-            af[first, :] = attention[:ROWS]
-            af[second, :] = attention[ROWS:]
+            for n, spot in enumerate(spots(g, c, i)):
+                af[spot, :] = attention[n * ROWS:(n + 1) * ROWS]
             return q, pb, jnp.concatenate(doss, axis=0), jnp.concatenate(dss, axis=0)
 
         def query_part(i, ds):
-            first, second = spots(g, c, i)
             dq = dot(ds, kcat[g, :wide, :]) * scale
-            dqf[first, :] = dq[:ROWS]
-            dqf[second, :] = dq[ROWS:]
+            for n, spot in enumerate(spots(g, c, i)):
+                dqf[spot, :] = dq[n * ROWS:(n + 1) * ROWS]
 
         def gradients(i, q, pb, dos, ds):
             if final:
@@ -293,7 +291,7 @@
     peers = lax.axis_size("seq") - 1
     chunks = rows_here // ROWS
     width = PAD + rows_here
-    pairs = per_kv // 2
+    pairs = per_kv // TOGETHER
     far = pl.BlockSpec(memory_space=pl.ANY)
     whole = pl.BlockSpec(memory_space=pltpu.VMEM)
     flat = jax.ShapeDtypeStruct((rows_here * heads_here, head_dim), jnp.bfloat16)
@@ -321,11 +319,11 @@
             pltpu.VMEM((ROWS, width), f32),
             pltpu.VMEM((kv_here, head_dim, width), f32),
             pltpu.VMEM((kv_here, head_dim, width), f32),
-            pltpu.VMEM((pairs, 2 * ROWS, chunks * (chunks + 1) // 2 * ROWS), f32),
-            pltpu.VMEM((pairs, 2 * ROWS, chunks * (chunks + 1) // 2 * ROWS), f32),
-            pltpu.VMEM((pairs, 2 * ROWS, width), bf16),
-            pltpu.VMEM((pairs, 2 * ROWS, width), bf16),
-            pltpu.VMEM((pairs, 2 * ROWS, head_dim), bf16),
+            pltpu.VMEM((pairs, TOGETHER * ROWS, chunks * (chunks + 1) // 2 * ROWS), f32),
+            pltpu.VMEM((pairs, TOGETHER * ROWS, chunks * (chunks + 1) // 2 * ROWS), f32),
+            pltpu.VMEM((pairs, TOGETHER * ROWS, width), bf16),
+            pltpu.VMEM((pairs, TOGETHER * ROWS, width), bf16),
+            pltpu.VMEM((pairs, TOGETHER * ROWS, head_dim), bf16),
             pltpu.VMEM((2 * kv_here * PMAX, head_dim), bf16),
             pltpu.VMEM((peers, 2 * kv_here * PMAX, head_dim), bf16),
             pltpu.VMEM((kv_here, PMAX, 2 * head_dim), bf16),

time: 40.9 us -> 40.6 us (level)
  no operation moved by 1% of the time
where the time goes in v5:
time: 40.6 us; the launch traced here: 40.4 us
  Pallas kernels  34.3 us (84%)
  local copies, waits for them, and re-layouts  5.42 us (13%)
  between operations  0.65 us (2%)
    pallas_call x1, Pallas kernels, body(): pl.pallas_call(functools.partial(attend, heads_here, kv_here, per_kv, chu...  34.3 us
    unnamed x9, local copies, waits for them, and re-layouts  5.42 us

profile of v5, /device:TPU:0, one launch (start us, length us, event | category | flops | bytes accessed | tf_op | source)
XLA Modules:
  0.0 40.4 jit_solution(10688448294369789503)
XLA Ops:
  0.6 0.0 copy-start
  0.6 0.7 %copy-done = s32[512]{0:T(512)S(1)} copy-done((s32[512]{0:T(512)S(1)}, s32[512]{0:T(512)}, u32[]{:S(2)}) %copy-start) | copy-done | bytes 2072
  1.3 0.0 copy-start.1
  1.3 0.7 %copy-done.1 = s32[8]{0:T(128)S(1)} copy-done((s32[8]{0:T(128)S(1)}, s32[8]{0:T(128)}, u32[]{:S(2)}) %copy-start.1) | copy-done | bytes 56
  2.0 0.0 copy-start.2
  2.0 0.7 %copy-done.2 = s32[8]{0:T(128)S(1)} copy-done((s32[8]{0:T(128)S(1)}, s32[8]{0:T(128)}, u32[]{:S(2)}) %copy-start.2) | copy-done | bytes 56
  2.6 34.3 %shard_map.85 = (bf16[8192,128]{1,0:T(8,128)(2,1)S(1)}, bf16[8192,128]{1,0:T(8,128)(2,1)S(1)}, bf16[512,512]{1,0:T(8,128)(2,1)S(1)}, bf16[64,512]{1,0:T(8,128)(2,1)}) custom-call(s32[8]{0:T(128)S(1)} %copy-done.1, s32[8]{0:T(128)S(1)} %copy-done.2, bf16[8192,128]{1,0:T(8,128)(2,1)} %bitcast.9, bf16[8192,128]{1,0:T(8,128)(2,1)} %bitcast.10, ...), custom_call_target="tpu_custom_call" | custom-call | tf_op jit(solution)/shard_map/pallas_call | solution.py:299
  36.9 1.3 %copy.12 = bf16[512,16,128]{2,1,0:T(8,128)(2,1)} copy(bf16[512,16,128]{2,1,0:T(8,128)(2,1)S(1)} %bitcast.7) | data formatting | bytes 4194304
  38.2 1.3 %copy.13 = bf16[512,16,128]{2,1,0:T(8,128)(2,1)} copy(bf16[512,16,128]{2,1,0:T(8,128)(2,1)S(1)} %bitcast.6) | data formatting | bytes 4194304
  39.6 0.8 %copy.14 = bf16[512,512]{1,0:T(8,128)(2,1)} copy(bf16[512,512]{1,0:T(8,128)(2,1)S(1)} %get-tuple-element.14) | data formatting | bytes 1048576
Async XLA Ops:
  0.6 0.7 %copy-start = (s32[512]{0:T(512)S(1)}, s32[512]{0:T(512)}, u32[]{:S(2)}) copy-start(s32[512]{0:T(512)} %param.9) | copy-start | bytes 6148
  1.3 0.7 %copy-start.1 = (s32[8]{0:T(128)S(1)}, s32[8]{0:T(128)}, u32[]{:S(2)}) copy-start(s32[8]{0:T(128)} %partner_ref.1) | copy-start | bytes 100
  2.0 0.7 %copy-start.2 = (s32[8]{0:T(128)S(1)}, s32[8]{0:T(128)}, u32[]{:S(2)}) copy-start(s32[8]{0:T(128)} %blocks_ref.1) | copy-start | bytes 100
